TPU v7x, 256 devices: a whole 4x4x8 slice. The times are simulated.
256 devices in a mesh: dp: 32 (over z_hi, x, core), tensor: 8 (over z_lo, y).
Axes of the slice: x: 4, y: 4, z: 8 (z_hi: 4, z_lo: 2; z = z_hi * 2 + z_lo), core: 2. Of those that a mesh axis runs over, the one named last changes fastest.
Arguments:
- gate_pre: bfloat16 [4096, 14336], P('dp', 'tensor'), may hold values from -6 to 6
- up_pre: bfloat16 [4096, 14336], P('dp', 'tensor'), may hold values from -6 to 6
- out_grad: bfloat16 [4096, 8192], P('dp', 'tensor'), may hold values from -5 to 5, as said below
- other_sq: float32 [64], P('dp'), may hold values from 0.0625 to 0.5
- added_noise: bfloat16 [8192, 14336], P('dp', 'tensor'), may hold values from -0.59765625 to 0.59765625
Outputs:
- down_grad: float32 [8192, 14336], P('dp', 'tensor')
- clip_factor: float32 [64], P('dp')
Inputs may be any that keep to these rules, and one draw needn't show every extreme that they name: `out_grad`: each example's rows share one scale.
All inputs are finite; a program needn't handle non-finite values.
Results may differ from a plain program's by a relative error of at most 0.0016.
Values may be sent and summed in bfloat16 or wider, within the bound.
No kernel may reach another device: no remote copies, remote signals or barrier semaphores. Data moves between devices by JAX's collectives and lax.ppermute only.
A program may use at most 128 MiB of HBM per device.

v0:
```python
import jax
import jax.numpy as jnp
from jax import lax
from jax.sharding import PartitionSpec as P

D = 8192
FF = 14336


def per_device(gate_pre, up_pre, out_grad, other_sq, added_noise):
    ex_local = other_sq.shape[0]
    tok_local = out_grad.shape[0]
    tok_each = tok_local // ex_local
    hidden = (jax.nn.silu(gate_pre.astype(jnp.float32)) * up_pre.astype(jnp.float32)).astype(
        jnp.bfloat16
    )
    hidden_blocks = hidden.reshape(ex_local, tok_each, hidden.shape[1])
    hidden_part = jnp.einsum(
        "btf,buf->btu", hidden_blocks, hidden_blocks, preferred_element_type=jnp.float32
    )
    full_grad = lax.all_gather(out_grad, "tensor", axis=1, tiled=True)
    hidden_gram = lax.psum(hidden_part, "tensor")
    grad_blocks = full_grad.reshape(ex_local, tok_each, full_grad.shape[1])
    grad_gram = jnp.einsum(
        "btf,buf->btu", grad_blocks, grad_blocks, preferred_element_type=jnp.float32
    )
    down_sq = jnp.sum(hidden_gram * grad_gram, axis=(1, 2))
    weight_count = jnp.float32(D) * jnp.float32(FF)
    clip_factor = jnp.minimum(
        jnp.float32(1.0), jnp.float32(1.0) / jnp.sqrt(down_sq / weight_count + other_sq)
    )
    token_factor = jnp.repeat(clip_factor, tok_each)
    scaled_local = (token_factor[:, None] * full_grad.astype(jnp.float32)).astype(jnp.bfloat16)
    scaled = lax.all_to_all(scaled_local, "dp", split_axis=1, concat_axis=0, tiled=True)
    examples_all = scaled.shape[0] // tok_each
    product = lax.dot_general(
        scaled,
        lax.all_gather(hidden, "dp", axis=0, tiled=True),
        (((0,), (0,)), ((), ())),
        preferred_element_type=jnp.float32,
    )
    down_grad = product / jnp.float32(examples_all) + added_noise.astype(jnp.float32)
    return (down_grad, clip_factor)


def solution(mesh):
    in_specs = (P("dp", "tensor"), P("dp", "tensor"), P("dp", "tensor"), P("dp"), P("dp", "tensor"))
    out_specs = (P("dp", "tensor"), P("dp"))
    return jax.shard_map(
        per_device, mesh=mesh, in_specs=in_specs, out_specs=out_specs, check_vma=False
    )
```

profile of v0, /device:TPU:35, one launch (start us, length us, event | category | flops | bytes accessed | tf_op | source)
XLA Modules:
  0.0 224.5 jit_solution(9717045769434128945)
XLA Ops:
  7.2 0.0 all-gather.3.cloned.1.call-start
  7.2 1.8 copy.7
  9.0 0.0 all-gather.3.cloned.1.call-update
  9.0 0.0 all-gather.5.cloned.1.call-start
  9.1 2.2 fusion.6
  11.3 0.0 all-gather.5.cloned.1.call-update
  11.3 1.4 fusion.7
  12.7 27.8 %psum.7 = f32[2,64,64]{2,1,0:T(8,128)S(1)} all-reduce(f32[2,64,64]{2,1,0:T(8,128)S(1)} %fusion.7), channel_id=1, replica_groups=mesh['dp'=32,'tensor'=8] {'tensor'}, use_global_device_ids=true, to_apply=%region_0.1 | all-reduce | flops 8192 | bytes 65536 | tf_op jit(solution)/shard_map/psum | solution.py:22
  40.6 9.8 %all-gather.3.cloned.1.call-done = bf16[128,8192]{0,1:T(8,128)(2,1)} async-done(((bf16[128,1024]{0,1:T(8,128)(2,1)}), bf16[128,8192]{0,1:T(8,128)(2,1)}) %all-gather.3.cloned.1.call-update) | async-done | bytes 2097168 | tf_op jit(solution)/shard_map/all_gather | solution.py:21
  50.4 2.9 %copy.8 = bf16[128,8192]{1,0:T(8,128)(2,1)S(1)} copy(bf16[128,8192]{0,1:T(8,128)(2,1)} %all-gather.3.cloned.1.call-done) | data formatting | bytes 4194304 | tf_op jit(solution)/shard_map/all_gather | solution.py:21
  53.3 0.0 copy-start.1
  53.3 0.8 fusion.1
  54.1 0.0 copy-done.1
  54.1 0.0 copy-start.2
  54.1 0.1 broadcast_in_dim.3
  54.2 0.1 mul.23
  54.3 2.0 multiply_convert_fusion
  56.3 0.0 copy-done.2
  56.3 79.8 %all_to_all.19 = bf16[128,32,256]{0,2,1:T(8,128)(2,1)} all-to-all(bf16[128,32,256]{0,2,1:T(8,128)(2,1)S(1)} %bitcast.13), channel_id=1, replica_groups=mesh['dp'=32,'tensor'=8] {'dp'}, dimensions={1} | all-to-all | bytes 4194304 | tf_op jit(solution)/shard_map/all_to_all | solution.py:34
  136.1 0.0 copy-start
  136.1 3.3 %copy.9 = bf16[32,128,256]{2,1,0:T(8,128)(2,1)S(1)} copy(bf16[32,128,256]{1,2,0:T(8,128)(2,1)} %bitcast.14) | data formatting | bytes 4194304 | tf_op jit(solution)/shard_map/all_to_all | solution.py:34
  139.5 69.5 %all-gather.5.cloned.1.call-done = bf16[4096,1792]{1,0:T(8,128)(2,1)} async-done(((bf16[128,1792]{1,0:T(8,128)(2,1)}), bf16[4096,1792]{1,0:T(8,128)(2,1)}) %all-gather.5.cloned.1.call-update) | async-done | bytes 14680080 | tf_op jit(solution)/shard_map/all_gather | solution.py:38
  208.9 0.0 copy-done
  208.9 8.7 %fusion = f32[256,1792]{1,0:T(8,128)} fusion(bf16[4096,256]{1,0:T(8,128)(2,1)S(1)} %bitcast.12, bf16[4096,1792]{1,0:T(8,128)(2,1)} %all-gather.5.cloned.1.call-done, bf16[256,1792]{1,0:T(8,128)(2,1)S(1)} %copy-done), kind=kOutput, calls=%fused_computation.2 | convolution fusion | flops 3759472640 | bytes 19529728 | tf_op jit(solution)/shard_map/dot_general | solution.py:36
  (1 shorter events, 0.0 us)
Async XLA Ops:
  7.2 43.3 %all-gather.3.cloned.1.call-start = ((), (), s32[]{:S(2)}) async-start(), calls=%async_computation.1 | async-start | bytes 2359296 | tf_op jit(solution)/shard_map/all_gather | solution.py:21
  9.0 199.9 %all-gather.5.cloned.1.call-start = ((), (), s32[]{:S(2)}) async-start(), calls=%async_computation.2 | async-start | bytes 15138816 | tf_op jit(solution)/shard_map/all_gather | solution.py:38
  53.3 0.8 copy-start.1
  54.1 2.2 copy-start.2
  136.1 72.8 %copy-start = (bf16[256,1792]{1,0:T(8,128)(2,1)S(1)}, bf16[256,1792]{1,0:T(8,128)(2,1)}, u32[]{:S(2)}) copy-start(bf16[256,1792]{1,0:T(8,128)(2,1)} %param.9) | copy-start | bytes 2752516
Sparse Core Ops, SparseCore 0:
  9.8 40.5 all-gather.2
  53.5 155.3 all-gather.4
where the time goes:
time: 225 us; the launch traced here: 224 us
  blocking collectives  108 us (48%)
  waiting for transfers between devices  79.3 us (35%)
  between operations  14.1 us (6%)
  matrix products  10.9 us (5%)
  local copies, waits for them, and re-layouts  8.2 us (4%)
  other arithmetic  4.21 us (2%)
    all_to_all x1, blocking collectives, per_device(): lax.all_to_all(scaled_local, 'dp', split_axis=1, concat_axis=0, tiled=True)  79.8 us
    all_gather x1, waiting for transfers between devices, per_device(): lax.all_gather(hidden, 'dp', axis=0, tiled=True)  69.5 us
    psum x1, blocking collectives, per_device(): hidden_gram = lax.psum(hidden_part, 'tensor')  27.8 us
    all_gather x1, waiting for transfers between devices, per_device(): full_grad = lax.all_gather(out_grad, 'tensor', axis=1, tiled=True)  9.84 us
    dot_general x1, matrix products, per_device(): lax.dot_general(scaled, lax.all_gather(hidden, 'dp', axis=0, tiled=True),...  8.71 us
  transfers between devices with their start and end apart: 2, of which 2 were waited for; matrix products, arithmetic and copies ran while one was open for 6% of the time, Pallas kernels for 0%

commit v1 on v0

v1 whole, which is shorter than its diff:
```python
import jax
import jax.numpy as jnp
from jax import lax
from jax.experimental import pallas as pl
from jax.experimental.pallas import tpu as pltpu
from jax.sharding import PartitionSpec as P

D = 8192
FF = 14336
TILE = 256

DEVICES = [
    (zh, x, c, zl, y)
    for zh in range(4)
    for x in range(4)
    for c in range(2)
    for zl in range(2)
    for y in range(4)
]


def index(zh, x, c, zl, y):
    return (((zh % 4) * 4 + x % 4) * 2 + c % 2) * 8 + (zl % 2) * 4 + y % 4


def permute(value, to):
    pairs = [(index(*d), index(*to(*d))) for d in DEVICES]
    return lax.ppermute(value, ("dp", "tensor"), pairs)


def send(value, zh=0, x=0, c=0, zl=0, y=0):
    return permute(value, lambda z_, x_, c_, l_, y_: (z_ + zh, x_ + x, c_ + c, l_ + zl, y_ + y))


def pick(stacked, at):
    return lax.dynamic_index_in_dim(stacked, at, 0, keepdims=False)


def product_kernel(pieces, places_ref, clip_ref, *refs):
    n = len(pieces)
    ring_refs, piece_refs, refs = refs[:4], refs[4 : 4 + n], refs[4 + n :]
    theirs_ref, mine_ref, ring, scaled, hidden, acc, ring_sem, sem, out_sem = refs
    copies = [pltpu.make_async_copy(ring_refs[r], ring.at[r], ring_sem.at[r]) for r in range(4)]
    for p, (to, start, rows) in enumerate(pieces):
        copies.append(
            pltpu.make_async_copy(
                piece_refs[p].at[pl.ds(start, rows)], hidden.at[pl.ds(to, rows)], sem.at[p]
            )
        )
    for copy in copies:
        copy.start()
    core, l_at, y_at = places_ref[16], places_ref[17], places_ref[18]
    for copy in copies[:4]:
        copy.wait()
    halves = [pl.ds(pl.multiple_of(h * 256, 256), 256) for h in (1 - core, core)]
    for r in range(4):
        y = (y_at + 4 - r) % 4
        for o in range(2):
            l = l_at if o == 0 else 1 - l_at
            part = (l * 4 + y) * 16

            @pl.loop(0, 16)
            def _(j):
                block = places_ref[j]
                rows = pl.ds(pl.multiple_of(block * 16, 16), 16)
                to = pl.ds(pl.multiple_of(j * 128 + part, 16), 16)
                factor = clip_ref[block * 2 + l]
                for k in range(2):
                    value = ring[r, o, rows, halves[k]].astype(jnp.float32) * factor
                    scaled[to, k * 256 : (k + 1) * 256] = value.astype(jnp.bfloat16)

    for copy in copies[4:]:
        copy.wait()
    outs = []
    for i in range(hidden.shape[1] // TILE):
        at = pl.ds(i * TILE, TILE)
        acc[:, at] = lax.dot_general(
            scaled[...], hidden[:, at], (((0,), (0,)), ((), ())), preferred_element_type=jnp.float32
        )
        for k, out_ref in enumerate((theirs_ref, mine_ref)):
            outs.append(
                pltpu.make_async_copy(
                    acc.at[pl.ds(k * 256, 256), at], out_ref.at[:, at], out_sem.at[k, i]
                )
            )
            outs[-1].start()
    for copy in outs:
        copy.wait()


def pieces_of(h, keys, tok):
    arrays, layout = [], []
    for blk, key in enumerate(keys):
        to = blk * tok
        for array, start, rows in h[key]:
            arrays.append(array)
            layout.append((to, start, rows))
            to += rows
    return arrays, layout


HBM = pl.BlockSpec(memory_space=pltpu.HBM)
VMEM = pl.BlockSpec(memory_space=pltpu.VMEM)
SMEM = pl.BlockSpec(memory_space=pltpu.SMEM)
PARAMS = pltpu.CompilerParams(vmem_limit_bytes=60 << 20)
COST = pl.CostEstimate(flops=1 << 20, bytes_accessed=1 << 20, transcendentals=0)


def product(h, keys, ring, places, clips):
    tok = 128
    arrays, layout = pieces_of(h, keys, tok)
    ff = arrays[0].shape[1]
    return pl.pallas_call(
        lambda *refs: product_kernel(layout, *refs),
        out_shape=[jax.ShapeDtypeStruct((256, ff), jnp.float32)] * 2,
        in_specs=[SMEM, SMEM] + [HBM] * (4 + len(arrays)),
        out_specs=[HBM, HBM],
        scratch_shapes=[
            pltpu.VMEM((4,) + ring[0].shape, jnp.bfloat16),
            pltpu.VMEM((16 * tok, 512), jnp.bfloat16),
            pltpu.VMEM((16 * tok, ff), jnp.bfloat16),
            pltpu.VMEM((512, ff), jnp.float32),
            pltpu.SemaphoreType.DMA((4,)),
            pltpu.SemaphoreType.DMA((len(arrays),)),
            pltpu.SemaphoreType.DMA((2, ff // TILE)),
        ],
        compiler_params=PARAMS,
        cost_estimate=COST,
    )(places, clips, *ring, *arrays)


def split3(value):
    parts = []
    for _ in range(3):
        part = lax.reduce_precision(value, 8, 7)
        parts.append(part.astype(jnp.bfloat16))
        value = value - part
    return parts


def step(inputs, done):
    return lax.optimization_barrier((tuple(inputs), tuple(done)))[0]


def per_device(gate_pre, up_pre, out_grad, other_sq, added_noise):
    dp_at, t_at = lax.axis_index("dp"), lax.axis_index("tensor")
    z_at, x_at, c_at = dp_at // 8, (dp_at // 2) % 4, dp_at % 2
    l_at, y_at = t_at // 4, t_at % 4
    tok, ff = gate_pre.shape
    examples, ex = 64, 2

    def ring_x(value):
        return permute(value, lambda z, x, c, l, y: (z, x + 1 - 2 * c, c, l, y))

    def ring_z(value, way=1):
        return permute(value, lambda z, x, c, l, y: (z + way * (1 - 2 * c), x, c, l, y))

    hidden = (jax.nn.silu(gate_pre.astype(jnp.float32)) * up_pre.astype(jnp.float32)).astype(
        jnp.bfloat16
    )
    hidden_blocks = hidden.reshape(ex, tok // ex, ff)
    grad_blocks = out_grad.reshape(ex, tok // ex, out_grad.shape[1])
    grams = jnp.stack(
        [
            jnp.einsum("btf,buf->btu", v, v, preferred_element_type=jnp.float32)
            for v in (hidden_blocks, grad_blocks)
        ]
    )
    rows = grams.reshape(2, ex, 8, 8, 64).transpose(2, 0, 1, 3, 4).reshape(8, 2, 1024)
    message = jnp.concatenate(
        [out_grad.reshape(8, 16, 1024)] + split3(rows) + [jnp.zeros((8, 2, 1024), jnp.bfloat16)], axis=1
    )

    h = {(0, 0): [(hidden, 0, tok)]}
    z = ring_z(hidden)
    x = ring_x(hidden)
    h[0, 1] = [(x, 0, tok)]
    x = ring_x(x)
    h[1, 0], h[0, 2] = [(z, 0, tok)], [(x, 0, tok)]
    message = lax.all_to_all(message, "tensor", 0, 0, tiled=True)
    x = jnp.concatenate([x, z])
    z, x, message = step((z, x, message), ())
    z = ring_z(z)
    x = ring_x(x)
    h[2, 0], h[0, 3], h[1, 1] = [(z, 0, tok)], [(x, 0, tok)], [(x, tok, tok)]
    rows = jnp.sum(message[:, 16:22].astype(jnp.float32).reshape(8, 3, 2048), axis=(0, 1))
    rows = rows.reshape(2, ex, 8 * 64)
    weight_count = jnp.float32(D) * jnp.float32(FF)
    part = jnp.sum(rows[0] * rows[1], axis=1) / weight_count
    part = part + jnp.where(t_at == 0, other_sq, jnp.zeros_like(other_sq))
    lanes = jnp.repeat(part, 256)[None, :]
    extra = jnp.concatenate(split3(lanes) + [jnp.zeros((5, 512), jnp.bfloat16)])
    own = message[:, :16].reshape(8, 16, 2, 512).transpose(0, 2, 1, 3).reshape(16, 16, 512)
    message = jnp.concatenate([own, jnp.broadcast_to(extra[None], (16, 8, 512))], axis=1)
    groups = [[zx * 2 + c for zx in range(16)] for c in range(2)]
    message = lax.all_to_all(message, "dp", 0, 0, axis_index_groups=groups, tiled=True)
    across = x[:tok]
    x = jnp.concatenate([x[tok:], z])
    z, x, across = step((z, x, across), ())
    z = ring_z(z)
    x = ring_x(x)
    h[3, 0], h[1, 2], h[2, 1] = [(z, 0, tok)], [(x, 0, tok)], [(x, tok, tok)]
    extra = message[:, 16:19].reshape(16, 3, 2, 256)[:, :, :, :64].transpose(0, 2, 1, 3).reshape(16, 384)
    own = jnp.concatenate(
        [message[:, :16].reshape(256, 512), jnp.pad(extra, ((0, 0), (0, 128)))]
    )
    pair = jnp.stack([own, send(own, zl=1)])
    third = x[:tok]
    x = jnp.concatenate([x[tok:], z])
    x, across, pair = step((x, across, pair), ())
    z = ring_z(across, -1)
    x = ring_x(x)
    h[3, 3], h[2, 2], h[3, 1] = [(z, 0, tok)], [(x, 0, tok)], [(x, tok, tok)]
    ring = [pair, send(pair, y=1), None, send(pair, y=3)]
    x = jnp.concatenate([x[tok:], third])
    z, x, pair = step((z, x, pair), (ring[1], ring[3]))
    z = ring_z(z, -1)
    x = ring_x(x)
    h[2, 3], h[3, 2], h[1, 3] = [(z, 0, tok)], [(x, 0, tok)], [(x, tok, tok)]
    ring[2] = send(pair, y=2)

    total = sum(piece[:, 256:].astype(jnp.float32).sum(0) for piece in ring)
    total = total[:, :384].reshape(16, ex, 3, 64)[:, :, :, 0].sum(2)
    clips = jnp.minimum(jnp.float32(1.0), jnp.float32(1.0) / jnp.sqrt(total))
    clip_factor = pick(clips, z_at * 4 + x_at)
    keys = [(dz, dx) for dz in range(4) for dx in range(4)]
    way = 1 - 2 * c_at
    places = [((z_at - way * dz) % 4) * 4 + (x_at - way * dx) % 4 for dz, dx in keys]
    places = jnp.stack(places + [c_at, l_at, y_at])
    theirs, mine = product(h, keys, ring, places, clips.reshape(32))
    total = mine + send(theirs, c=1)
    down_grad = total / jnp.float32(examples) + added_noise.astype(jnp.float32)
    return (down_grad, clip_factor)


def solution(mesh):
    in_specs = (P("dp", "tensor"), P("dp", "tensor"), P("dp", "tensor"), P("dp"), P("dp", "tensor"))
    out_specs = (P("dp", "tensor"), P("dp"))
    return jax.shard_map(
        per_device, mesh=mesh, in_specs=in_specs, out_specs=out_specs, check_vma=False
    )
```

time: 225 us -> 138 us (0.61)
  the two profiles are of different devices: /device:TPU:35 before, /device:TPU:1 now
where the time goes in v1:
time: 138 us
  waiting for transfers between devices  54.6 us (40%)
  starting transfers between devices  52.2 us (38%)
  Pallas kernels  11.4 us (8%)
  other arithmetic  9.37 us (7%)
  local copies, waits for them, and re-layouts  7.77 us (6%)
  matrix products  1.48 us (1%)
    ppermute x16, waiting for transfers between devices, permute(): return lax.ppermute(value, ('dp', 'tensor'), pairs)  47.6 us
    ppermute x16, starting transfers between devices, permute(): return lax.ppermute(value, ('dp', 'tensor'), pairs)  38.1 us
    pallas_call x1, Pallas kernels, product(): pl.pallas_call(lambda *refs: product_kernel(layout, *refs), out_shape=[ja...  11.4 us
    all_to_all x1, starting transfers between devices, per_device(): lax.all_to_all(message, 'dp', 0, 0, axis_index_groups=groups, tiled=True)  8.56 us
    all_to_all x1, waiting for transfers between devices, per_device(): message = lax.all_to_all(message, 'tensor', 0, 0, tiled=True)  7.01 us
    all_to_all x1, starting transfers between devices, per_device(): message = lax.all_to_all(message, 'tensor', 0, 0, tiled=True)  5.54 us
    add x1, other arithmetic, per_device(): down_grad = total / jnp.float32(examples) + added_noise.astype(jnp.float32)  2.98 us
  transfers between devices with their start and end apart: 18, of which 8 were waited for; matrix products, arithmetic and copies ran while one was open for 8% of the time, Pallas kernels for 0%

profile of v1, /device:TPU:1, one launch (start us, length us, event | category | flops | bytes accessed | tf_op | source)
XLA Modules:
  0.0 137.9 jit_solution(49757920586348192)
XLA Ops:
  0.6 1.5 %fusion.4.refs_6_ = bf16[128,1792]{1,0:T(8,128)(2,1)S(1)} fusion(bf16[128,1792]{1,0:T(8,128)(2,1)} %param.6, bf16[128,1792]{1,0:T(8,128)(2,1)} %param.5), kind=kLoop, calls=%fused_computation.13 | loop fusion | flops 1835008 | bytes 1376256 | tf_op jit(solution)/shard_map/convert_element_type | solution.py:158
  2.1 3.4 %collective-permute-start.1 = (bf16[128,1792]{1,0:T(8,128)(2,1)S(1)}, bf16[128,1792]{1,0:T(8,128)(2,1)S(1)}, u32[]{:S(2)}, u32[]{:S(2)}) collective-permute-start(bf16[128,1792]{1,0:T(8,128)(2,1)S(1)} %fusion.4.refs_6_), channel_id=1, source_target_pairs={{0,16},{1,17},{2,18},{3,19},{4,20},{5,21},{6,22},{7,23},{8,56},{9,... | collective-permute-start | bytes 1376264 | tf_op jit(solution)/shard_map/ppermute | solution.py:28
  5.5 6.0 %collective-permute-start = (bf16[128,1792]{1,0:T(8,128)(2,1)S(1)}, bf16[128,1792]{1,0:T(8,128)(2,1)S(1)}, u32[]{:S(2)}, u32[]{:S(2)}) collective-permute-start(bf16[128,1792]{1,0:T(8,128)(2,1)S(1)} %fusion.4.refs_6_), channel_id=1, source_target_pairs={{0,64},{1,65},{2,66},{3,67},{4,68},{5,69},{6,70},{7,71},{8,200},{9... | collective-permute-start | bytes 1376264 | tf_op jit(solution)/shard_map/ppermute | solution.py:28
  11.5 1.2 convolution_bitcast_fusion.1
  13.2 1.2 collective-permute-start.2
  14.6 1.6 %concatenate.29 = bf16[8,24,1024]{2,1,0:T(8,128)(2,1)} concatenate(bf16[8,16,1024]{2,1,0:T(8,128)(2,1)S(1)} %bitcast.52, bf16[8,2,1024]{2,1,0:T(2,128)(2,1)S(1)} %copy.14, bf16[8,2,1024]{2,1,0:T(2,128)(2,1)S(1)} %copy.15, bf16[8,2,1024]{2,1,0:T(2,128)(2,1)S(1)} %copy.16, bf16[8,2,1024]{2,1,0:T(2,128)(2,1)S(1)} %broadcast_in_dim.15), dimensions={1} | concatenate | bytes 786432 | tf_op jit(solution)/shard_map/concatenate | solution.py:170
  16.2 5.5 %all-to-all-start = ((bf16[8,24,1024]{2,1,0:T(8,128)(2,1)}), bf16[8,24,1024]{2,1,0:T(8,128)(2,1)S(1)}, u32[]{:S(2)}, u32[]{:S(2)}) async-start(bf16[8,24,1024]{2,1,0:T(8,128)(2,1)} %concatenate.29), calls=%async_computation | async-start | bytes 786432 | tf_op jit(solution)/shard_map/all_to_all | solution.py:180
  21.9 1.1 pad_maximum_fusion
  23.0 7.0 %all-to-all-done = bf16[8,24,1024]{2,1,0:T(8,128)(2,1)S(1)} async-done(((bf16[8,24,1024]{2,1,0:T(8,128)(2,1)}), bf16[8,24,1024]{2,1,0:T(8,128)(2,1)S(1)}, u32[]{:S(2)}, u32[]{:S(2)}) %all-to-all-start) | async-done | bytes 393248 | tf_op jit(solution)/shard_map/all_to_all | solution.py:180
  30.5 0.8 pad_maximum_fusion.5
  31.3 8.6 %all-to-all-start.1 = ((bf16[16,24,512]{2,1,0:T(8,128)(2,1)}), bf16[16,24,512]{2,1,0:T(8,128)(2,1)S(1)}, u32[]{:S(2)}, u32[]{:S(2)}) async-start(bf16[16,24,512]{2,1,0:T(8,128)(2,1)} %pad_maximum_fusion.5), calls=%async_computation.1 | async-start | bytes 786432 | tf_op jit(solution)/shard_map/all_to_all | solution.py:196
  39.8 3.6 %collective-permute-start.3 = (bf16[128,1792]{1,0:T(8,128)(2,1)S(1)}, bf16[128,1792]{1,0:T(8,128)(2,1)S(1)}, u32[]{:S(2)}, u32[]{:S(2)}) collective-permute-start(bf16[128,1792]{1,0:T(8,128)(2,1)S(1)} %collective-permute-done.refs_10_), channel_id=1, source_target_pairs={{0,64},{1,65},{2,66},{3,67},{4,68},{5,69},{6,70},{7,71},{8,200},{9... | collective-permute-start | bytes 1376264 | tf_op jit(solution)/shard_map/ppermute | solution.py:28
  43.4 0.9 fusion.14
  44.3 17.2 %collective-permute-done.3.refs_14_ = bf16[128,1792]{1,0:T(8,128)(2,1)S(1)} collective-permute-done((bf16[128,1792]{1,0:T(8,128)(2,1)S(1)}, bf16[128,1792]{1,0:T(8,128)(2,1)S(1)}, u32[]{:S(2)}, u32[]{:S(2)}) %collective-permute-start.3) | collective-permute-done | bytes 458784 | tf_op jit(solution)/shard_map/ppermute | solution.py:28
  61.6 2.5 %collective-permute-start.5 = (bf16[256,1792]{1,0:T(8,128)(2,1)S(1)}, bf16[256,1792]{1,0:T(8,128)(2,1)S(1)}, u32[]{:S(2)}, u32[]{:S(2)}) collective-permute-start(bf16[256,1792]{1,0:T(8,128)(2,1)S(1)} %pad_maximum_fusion.1), channel_id=1, source_target_pairs={{0,16},{1,17},{2,18},{3,19},{4,20},{5,21},{6,22},{7,23},{8,56},{9,... | collective-permute-start | bytes 2752520 | tf_op jit(solution)/shard_map/ppermute | solution.py:28
  64.5 2.3 %collective-permute-start.6 = (bf16[128,1792]{1,0:T(8,128)(2,1)S(1)}, bf16[128,1792]{1,0:T(8,128)(2,1)S(1)}, u32[]{:S(2)}, u32[]{:S(2)}) collective-permute-start(bf16[128,1792]{1,0:T(8,128)(2,1)S(1)} %collective-permute-done.3.refs_14_), channel_id=1, source_target_pairs={{0,64},{1,65},{2,66},{3,67},{4,68},{5,69},{6,70},{7,71},{8,200},{9... | collective-permute-start | bytes 1376264 | tf_op jit(solution)/shard_map/ppermute | solution.py:28
  66.8 10.5 %collective-permute-done.7 = bf16[272,512]{1,0:T(8,128)(2,1)S(1)} collective-permute-done((bf16[272,512]{1,0:T(8,128)(2,1)S(1)}, bf16[272,512]{1,0:T(8,128)(2,1)S(1)}, u32[]{:S(2)}, u32[]{:S(2)}) %collective-permute-start.7) | collective-permute-done | bytes 278560 | tf_op jit(solution)/shard_map/ppermute | solution.py:28
  78.5 1.2 collective-permute-start.11
  80.0 3.4 %collective-permute-start.9 = (bf16[128,1792]{1,0:T(8,128)(2,1)S(1)}, bf16[128,1792]{1,0:T(8,128)(2,1)S(1)}, u32[]{:S(2)}, u32[]{:S(2)}) collective-permute-start(bf16[128,1792]{1,0:T(8,128)(2,1)S(1)} %copy-done.12), channel_id=1, source_target_pairs={{0,192},{1,193},{2,194},{3,195},{4,196},{5,197},{6,198},{7,199},{8... | collective-permute-start | bytes 1376264 | tf_op jit(solution)/shard_map/ppermute | solution.py:28
  83.3 7.6 %collective-permute-done.10.refs_16_.refs_19_ = bf16[256,1792]{1,0:T(8,128)(2,1)S(1)} collective-permute-done((bf16[256,1792]{1,0:T(8,128)(2,1)S(1)}, bf16[256,1792]{1,0:T(8,128)(2,1)S(1)}, u32[]{:S(2)}, u32[]{:S(2)}) %collective-permute-start.10) | collective-permute-done | bytes 917536 | tf_op jit(solution)/shard_map/ppermute | solution.py:28
  91.1 0.9 copy-done.14
  92.0 1.7 %collective-permute-start.12 = (bf16[2,272,512]{2,1,0:T(8,128)(2,1)S(1)}, bf16[2,272,512]{2,1,0:T(8,128)(2,1)}, u32[]{:S(2)}, u32[]{:S(2)}) collective-permute-start(bf16[2,272,512]{2,1,0:T(8,128)(2,1)S(1)} %pad_maximum_fusion.4.refs_2_), channel_id=1, source_target_pairs={{0,2},{1,3},{2,0},{3,1},{4,6},{5,7},{6,4},{7,5},{8,10},{9,11},{10,... | collective-permute-start | bytes 1671176 | tf_op jit(solution)/shard_map/ppermute | solution.py:28
  94.4 0.8 collective-permute-start.13
  95.2 0.8 convert_reduce_fusion.1
  96.0 0.8 convert_reduce_fusion.3
  96.8 4.6 %collective-permute-start.14 = (bf16[128,1792]{1,0:T(8,128)(2,1)}, bf16[128,1792]{1,0:T(8,128)(2,1)}, u32[]{:S(2)}, u32[]{:S(2)}) collective-permute-start(bf16[128,1792]{1,0:T(8,128)(2,1)} %copy-done.14), channel_id=1, source_target_pairs={{0,192},{1,193},{2,194},{3,195},{4,196},{5,197},{6,198},{7,199},{8... | collective-permute-start | bytes 1376264 | tf_op jit(solution)/shard_map/ppermute | solution.py:28
  103.7 8.3 %collective-permute-done.14.refs_17_ = bf16[128,1792]{1,0:T(8,128)(2,1)} collective-permute-done((bf16[128,1792]{1,0:T(8,128)(2,1)}, bf16[128,1792]{1,0:T(8,128)(2,1)}, u32[]{:S(2)}, u32[]{:S(2)}) %collective-permute-start.14) | collective-permute-done | bytes 458784 | tf_op jit(solution)/shard_map/ppermute | solution.py:28
  112.0 1.0 copy-done.4
  113.0 11.4 %shard_map.68 = (f32[256,1792]{1,0:T(8,128)}, f32[256,1792]{1,0:T(8,128)}) custom-call(s32[19]{0:T(128)} %stack.97.refs_0_, f32[32]{0:T(128)} %min.8.refs_1_, bf16[2,272,512]{2,1,0:T(8,128)(2,1)} %copy-done.5, bf16[2,272,512]{2,1,0:T(8,128)(2,1)} %collective-permute-done.8.refs_3_, bf16[2,272,512]{2,1,0:T(8,128)(2,1)} %collective-permute-done.12.refs_4_, ...), custom_call_target="tpu_custom_call" | custom-call | flops 1048576 | bytes 1048576 | tf_op jit(solution)/shard_map/pallas_call | solution.py:113
  124.4 6.9 %collective-permute-start.15 = (f32[256,1792]{1,0:T(8,128)}, f32[256,1792]{1,0:T(8,128)S(1)}, u32[]{:S(2)}, u32[]{:S(2)}) collective-permute-start(f32[256,1792]{1,0:T(8,128)} %get-tuple-element.29), channel_id=1, source_target_pairs={{0,8},{1,9},{2,10},{3,11},{4,12},{5,13},{6,14},{7,15},{8,0},{9,1},... | collective-permute-start | bytes 5505032 | tf_op jit(solution)/shard_map/ppermute | solution.py:28
  131.8 3.1 %collective-permute-done.15 = f32[256,1792]{1,0:T(8,128)S(1)} collective-permute-done((f32[256,1792]{1,0:T(8,128)}, f32[256,1792]{1,0:T(8,128)S(1)}, u32[]{:S(2)}, u32[]{:S(2)}) %collective-permute-start.15) | collective-permute-done | bytes 1835040 | tf_op jit(solution)/shard_map/ppermute | solution.py:28
  134.9 3.0 %convert_add_fusion = f32[256,1792]{1,0:T(8,128)} fusion(bf16[256,1792]{1,0:T(8,128)(2,1)S(1)} %copy-done.11, f32[256,1792]{1,0:T(8,128)} %get-tuple-element.28, f32[256,1792]{1,0:T(8,128)S(1)} %collective-permute-done.15), kind=kLoop, calls=%fused_computation | loop fusion | flops 1835008 | bytes 6422528 | tf_op jit(solution)/shard_map/add | solution.py:232
  (90 shorter events, 6.6 us)
Async XLA Ops:
  0.6 13.9 %copy-start.6 = (bf16[128,1024]{1,0:T(8,128)(2,1)S(1)}, bf16[128,1024]{1,0:T(8,128)(2,1)}, u32[]{:S(2)}) copy-start(bf16[128,1024]{1,0:T(8,128)(2,1)} %param.7) | copy-start | bytes 786436
  2.1 14.0 %copy-start.2 = (bf16[128,1792]{1,0:T(8,128)(2,1)}, bf16[128,1792]{1,0:T(8,128)(2,1)S(1)}, u32[]{:S(2)}) copy-start(bf16[128,1792]{1,0:T(8,128)(2,1)S(1)} %fusion.4.refs_6_) | copy-start | bytes 1376260
  2.1 11.0 %collective-permute-start.1 = (bf16[128,1792]{1,0:T(8,128)(2,1)S(1)}, bf16[128,1792]{1,0:T(8,128)(2,1)S(1)}, u32[]{:S(2)}, u32[]{:S(2)}) collective-permute-start(bf16[128,1792]{1,0:T(8,128)(2,1)S(1)} %fusion.4.refs_6_), channel_id=1, source_target_pairs={{0,16},{1,17},{2,18},{3,19},{4,20},{5,21},{6,22},{7,23},{8,56},{9,... | collective-permute-start | bytes 1376264 | tf_op jit(solution)/shard_map/ppermute | solution.py:28
  5.5 16.4 %collective-permute-start = (bf16[128,1792]{1,0:T(8,128)(2,1)S(1)}, bf16[128,1792]{1,0:T(8,128)(2,1)S(1)}, u32[]{:S(2)}, u32[]{:S(2)}) collective-permute-start(bf16[128,1792]{1,0:T(8,128)(2,1)S(1)} %fusion.4.refs_6_), channel_id=1, source_target_pairs={{0,64},{1,65},{2,66},{3,67},{4,68},{5,69},{6,70},{7,71},{8,200},{9... | collective-permute-start | bytes 1376264 | tf_op jit(solution)/shard_map/ppermute | solution.py:28
  13.2 9.8 %copy-start.13 = (bf16[128,1792]{1,0:T(8,128)(2,1)}, bf16[128,1792]{1,0:T(8,128)(2,1)S(1)}, u32[]{:S(2)}) copy-start(bf16[128,1792]{1,0:T(8,128)(2,1)S(1)} %collective-permute-done.1.refs_7_) | copy-start | bytes 1376260
  13.2 8.7 %collective-permute-start.2 = (bf16[128,1792]{1,0:T(8,128)(2,1)S(1)}, bf16[128,1792]{1,0:T(8,128)(2,1)S(1)}, u32[]{:S(2)}, u32[]{:S(2)}) collective-permute-start(bf16[128,1792]{1,0:T(8,128)(2,1)S(1)} %collective-permute-done.1.refs_7_), channel_id=1, source_target_pairs={{0,16},{1,17},{2,18},{3,19},{4,20},{5,21},{6,22},{7,23},{8,56},{9,... | collective-permute-start | bytes 1376264 | tf_op jit(solution)/shard_map/ppermute | solution.py:28
  14.5 15.7 %copy-start.15 = (f32[2]{0:T(128)S(1)}, f32[2]{0:T(128)}, u32[]{:S(2)}) copy-start(f32[2]{0:T(128)} %param.8) | copy-start | bytes 28
  16.2 13.8 %all-to-all-start = ((bf16[8,24,1024]{2,1,0:T(8,128)(2,1)}), bf16[8,24,1024]{2,1,0:T(8,128)(2,1)S(1)}, u32[]{:S(2)}, u32[]{:S(2)}) async-start(bf16[8,24,1024]{2,1,0:T(8,128)(2,1)} %concatenate.29), calls=%async_computation | async-start | bytes 786432 | tf_op jit(solution)/shard_map/all_to_all | solution.py:180
  21.9 18.0 %copy-start.7 = (bf16[128,1792]{1,0:T(8,128)(2,1)}, bf16[128,1792]{1,0:T(8,128)(2,1)S(1)}, u32[]{:S(2)}) copy-start(bf16[128,1792]{1,0:T(8,128)(2,1)S(1)} %collective-permute-done.refs_10_) | copy-start | bytes 1376260
  21.9 9.4 %copy-start.8 = (bf16[128,1792]{1,0:T(8,128)(2,1)}, bf16[128,1792]{1,0:T(8,128)(2,1)S(1)}, u32[]{:S(2)}) copy-start(bf16[128,1792]{1,0:T(8,128)(2,1)S(1)} %collective-permute-done.2.refs_8_) | copy-start | bytes 1376260
  30.3 13.1 %collective-permute-start.4 = (bf16[256,1792]{1,0:T(8,128)(2,1)}, bf16[256,1792]{1,0:T(8,128)(2,1)S(1)}, u32[]{:S(2)}, u32[]{:S(2)}) collective-permute-start(bf16[256,1792]{1,0:T(8,128)(2,1)} %pad_maximum_fusion), channel_id=1, source_target_pairs={{0,16},{1,17},{2,18},{3,19},{4,20},{5,21},{6,22},{7,23},{8,56},{9,... | collective-permute-start | bytes 2752520 | tf_op jit(solution)/shard_map/ppermute | solution.py:28
  31.3 32.9 %all-to-all-start.1 = ((bf16[16,24,512]{2,1,0:T(8,128)(2,1)}), bf16[16,24,512]{2,1,0:T(8,128)(2,1)S(1)}, u32[]{:S(2)}, u32[]{:S(2)}) async-start(bf16[16,24,512]{2,1,0:T(8,128)(2,1)} %pad_maximum_fusion.5), calls=%async_computation.1 | async-start | bytes 786432 | tf_op jit(solution)/shard_map/all_to_all | solution.py:196
  39.8 21.7 %collective-permute-start.3 = (bf16[128,1792]{1,0:T(8,128)(2,1)S(1)}, bf16[128,1792]{1,0:T(8,128)(2,1)S(1)}, u32[]{:S(2)}, u32[]{:S(2)}) collective-permute-start(bf16[128,1792]{1,0:T(8,128)(2,1)S(1)} %collective-permute-done.refs_10_), channel_id=1, source_target_pairs={{0,64},{1,65},{2,66},{3,67},{4,68},{5,69},{6,70},{7,71},{8,200},{9... | collective-permute-start | bytes 1376264 | tf_op jit(solution)/shard_map/ppermute | solution.py:28
  43.4 18.2 %copy-start = (bf16[256,1792]{1,0:T(8,128)(2,1)}, bf16[256,1792]{1,0:T(8,128)(2,1)S(1)}, u32[]{:S(2)}) copy-start(bf16[256,1792]{1,0:T(8,128)(2,1)S(1)} %collective-permute-done.4.refs_9_.refs_11_) | copy-start | bytes 2752516
  61.6 15.8 %copy-start.9 = (bf16[128,1792]{1,0:T(8,128)(2,1)}, bf16[128,1792]{1,0:T(8,128)(2,1)S(1)}, u32[]{:S(2)}) copy-start(bf16[128,1792]{1,0:T(8,128)(2,1)S(1)} %collective-permute-done.3.refs_14_) | copy-start | bytes 1376260
  61.6 15.7 %collective-permute-start.5 = (bf16[256,1792]{1,0:T(8,128)(2,1)S(1)}, bf16[256,1792]{1,0:T(8,128)(2,1)S(1)}, u32[]{:S(2)}, u32[]{:S(2)}) collective-permute-start(bf16[256,1792]{1,0:T(8,128)(2,1)S(1)} %pad_maximum_fusion.1), channel_id=1, source_target_pairs={{0,16},{1,17},{2,18},{3,19},{4,20},{5,21},{6,22},{7,23},{8,56},{9,... | collective-permute-start | bytes 2752520 | tf_op jit(solution)/shard_map/ppermute | solution.py:28
  64.4 12.9 %collective-permute-start.7 = (bf16[272,512]{1,0:T(8,128)(2,1)S(1)}, bf16[272,512]{1,0:T(8,128)(2,1)S(1)}, u32[]{:S(2)}, u32[]{:S(2)}) collective-permute-start(bf16[272,512]{1,0:T(8,128)(2,1)S(1)} %get-tuple-element.37), channel_id=1, source_target_pairs={{0,4},{1,5},{2,6},{3,7},{4,0},{5,1},{6,2},{7,3},{8,12},{9,13},{10,... | collective-permute-start | bytes 835592 | tf_op jit(solution)/shard_map/ppermute | solution.py:28
  64.5 13.0 %collective-permute-start.6 = (bf16[128,1792]{1,0:T(8,128)(2,1)S(1)}, bf16[128,1792]{1,0:T(8,128)(2,1)S(1)}, u32[]{:S(2)}, u32[]{:S(2)}) collective-permute-start(bf16[128,1792]{1,0:T(8,128)(2,1)S(1)} %collective-permute-done.3.refs_14_), channel_id=1, source_target_pairs={{0,64},{1,65},{2,66},{3,67},{4,68},{5,69},{6,70},{7,71},{8,200},{9... | collective-permute-start | bytes 1376264 | tf_op jit(solution)/shard_map/ppermute | solution.py:28
  77.4 17.8 %copy-start.5 = (bf16[2,272,512]{2,1,0:T(8,128)(2,1)}, bf16[2,272,512]{2,1,0:T(8,128)(2,1)S(1)}, u32[]{:S(2)}) copy-start(bf16[2,272,512]{2,1,0:T(8,128)(2,1)S(1)} %pad_maximum_fusion.4.refs_2_) | copy-start | bytes 1671172
  77.4 2.6 %copy-start.12 = (bf16[128,1792]{1,0:T(8,128)(2,1)S(1)}, bf16[128,1792]{1,0:T(8,128)(2,1)}, u32[]{:S(2)}) copy-start(bf16[128,1792]{1,0:T(8,128)(2,1)} %get-tuple-element.23) | copy-start | bytes 1376260
  77.5 13.6 %copy-start.10 = (bf16[128,1792]{1,0:T(8,128)(2,1)}, bf16[128,1792]{1,0:T(8,128)(2,1)S(1)}, u32[]{:S(2)}) copy-start(bf16[128,1792]{1,0:T(8,128)(2,1)S(1)} %collective-permute-done.6.refs_18_) | copy-start | bytes 1376260
  78.3 12.6 %collective-permute-start.10 = (bf16[256,1792]{1,0:T(8,128)(2,1)S(1)}, bf16[256,1792]{1,0:T(8,128)(2,1)S(1)}, u32[]{:S(2)}, u32[]{:S(2)}) collective-permute-start(bf16[256,1792]{1,0:T(8,128)(2,1)S(1)} %pad_maximum_fusion.2), channel_id=1, source_target_pairs={{0,16},{1,17},{2,18},{3,19},{4,20},{5,21},{6,22},{7,23},{8,56},{9,... | collective-permute-start | bytes 2752520 | tf_op jit(solution)/shard_map/ppermute | solution.py:28
  78.5 12.6 %collective-permute-start.11 = (bf16[2,272,512]{2,1,0:T(8,128)(2,1)S(1)}, bf16[2,272,512]{2,1,0:T(8,128)(2,1)}, u32[]{:S(2)}, u32[]{:S(2)}) collective-permute-start(bf16[2,272,512]{2,1,0:T(8,128)(2,1)S(1)} %pad_maximum_fusion.4.refs_2_), channel_id=1, source_target_pairs={{0,3},{1,0},{2,1},{3,2},{4,7},{5,4},{6,5},{7,6},{8,11},{9,8},{10,9... | collective-permute-start | bytes 1671176 | tf_op jit(solution)/shard_map/ppermute | solution.py:28
  79.7 11.4 %collective-permute-start.8 = (bf16[2,272,512]{2,1,0:T(8,128)(2,1)S(1)}, bf16[2,272,512]{2,1,0:T(8,128)(2,1)}, u32[]{:S(2)}, u32[]{:S(2)}) collective-permute-start(bf16[2,272,512]{2,1,0:T(8,128)(2,1)S(1)} %pad_maximum_fusion.4.refs_2_), channel_id=1, source_target_pairs={{0,1},{1,2},{2,3},{3,0},{4,5},{5,6},{6,7},{7,4},{8,9},{9,10},{10,1... | collective-permute-start | bytes 1671176 | tf_op jit(solution)/shard_map/ppermute | solution.py:28
  80.0 11.1 %collective-permute-start.9 = (bf16[128,1792]{1,0:T(8,128)(2,1)S(1)}, bf16[128,1792]{1,0:T(8,128)(2,1)S(1)}, u32[]{:S(2)}, u32[]{:S(2)}) collective-permute-start(bf16[128,1792]{1,0:T(8,128)(2,1)S(1)} %copy-done.12), channel_id=1, source_target_pairs={{0,192},{1,193},{2,194},{3,195},{4,196},{5,197},{6,198},{7,199},{8... | collective-permute-start | bytes 1376264 | tf_op jit(solution)/shard_map/ppermute | solution.py:28
  90.9 12.1 %copy-start.3 = (bf16[256,1792]{1,0:T(8,128)(2,1)}, bf16[256,1792]{1,0:T(8,128)(2,1)S(1)}, u32[]{:S(2)}) copy-start(bf16[256,1792]{1,0:T(8,128)(2,1)S(1)} %collective-permute-done.10.refs_16_.refs_19_) | copy-start | bytes 2752516
  92.0 10.1 %collective-permute-start.12 = (bf16[2,272,512]{2,1,0:T(8,128)(2,1)S(1)}, bf16[2,272,512]{2,1,0:T(8,128)(2,1)}, u32[]{:S(2)}, u32[]{:S(2)}) collective-permute-start(bf16[2,272,512]{2,1,0:T(8,128)(2,1)S(1)} %pad_maximum_fusion.4.refs_2_), channel_id=1, source_target_pairs={{0,2},{1,3},{2,0},{3,1},{4,6},{5,7},{6,4},{7,5},{8,10},{9,11},{10,... | collective-permute-start | bytes 1671176 | tf_op jit(solution)/shard_map/ppermute | solution.py:28
  94.4 17.7 %collective-permute-start.13 = (bf16[256,1792]{1,0:T(8,128)(2,1)S(1)}, bf16[256,1792]{1,0:T(8,128)(2,1)S(1)}, u32[]{:S(2)}, u32[]{:S(2)}) collective-permute-start(bf16[256,1792]{1,0:T(8,128)(2,1)S(1)} %pad_maximum_fusion.3), channel_id=1, source_target_pairs={{0,16},{1,17},{2,18},{3,19},{4,20},{5,21},{6,22},{7,23},{8,56},{9,... | collective-permute-start | bytes 2752520 | tf_op jit(solution)/shard_map/ppermute | solution.py:28
  96.8 15.3 %collective-permute-start.14 = (bf16[128,1792]{1,0:T(8,128)(2,1)}, bf16[128,1792]{1,0:T(8,128)(2,1)}, u32[]{:S(2)}, u32[]{:S(2)}) collective-permute-start(bf16[128,1792]{1,0:T(8,128)(2,1)} %copy-done.14), channel_id=1, source_target_pairs={{0,192},{1,193},{2,194},{3,195},{4,196},{5,197},{6,198},{7,199},{8... | collective-permute-start | bytes 1376264 | tf_op jit(solution)/shard_map/ppermute | solution.py:28
  103.7 31.2 %copy-start.11 = (bf16[256,1792]{1,0:T(8,128)(2,1)S(1)}, bf16[256,1792]{1,0:T(8,128)(2,1)}, u32[]{:S(2)}) copy-start(bf16[256,1792]{1,0:T(8,128)(2,1)} %param.9) | copy-start | bytes 2752516
  112.0 1.0 copy-start.4
  124.4 10.5 %collective-permute-start.15 = (f32[256,1792]{1,0:T(8,128)}, f32[256,1792]{1,0:T(8,128)S(1)}, u32[]{:S(2)}, u32[]{:S(2)}) collective-permute-start(f32[256,1792]{1,0:T(8,128)} %get-tuple-element.29), channel_id=1, source_target_pairs={{0,8},{1,9},{2,10},{3,11},{4,12},{5,13},{6,14},{7,15},{8,0},{9,1},... | collective-permute-start | bytes 5505032 | tf_op jit(solution)/shard_map/ppermute | solution.py:28
  (2 other events, 1.8 us)

commit v2 on v1

--- a/solution.py
+++ b/solution.py
@@ -7,7 +7,8 @@
 
 D = 8192
 FF = 14336
-TILE = 256
+TILE = 896
+GROUP = 512
 
 DEVICES = [
     (zh, x, c, zl, y)
@@ -36,54 +37,78 @@
     return lax.dynamic_index_in_dim(stacked, at, 0, keepdims=False)
 
 
-def product_kernel(pieces, places_ref, clip_ref, *refs):
+def product_kernel(pieces, tokens, places_ref, *refs):
     n = len(pieces)
-    ring_refs, piece_refs, refs = refs[:4], refs[4 : 4 + n], refs[4 + n :]
-    theirs_ref, mine_ref, ring, scaled, hidden, acc, ring_sem, sem, out_sem = refs
-    copies = [pltpu.make_async_copy(ring_refs[r], ring.at[r], ring_sem.at[r]) for r in range(4)]
-    for p, (to, start, rows) in enumerate(pieces):
-        copies.append(
-            pltpu.make_async_copy(
-                piece_refs[p].at[pl.ds(start, rows)], hidden.at[pl.ds(to, rows)], sem.at[p]
-            )
+    ring_refs, piece_refs, refs = refs[:4], refs[4 : 4 + n], refs[4 + n + tokens :]
+    theirs_ref, mine_ref, ring, factors, scaled, hidden, acc, ring_sem, sem, out_sem = refs
+    first = [pltpu.make_async_copy(ring_refs[r], ring.at[r], ring_sem.at[r]) for r in range(4)]
+    for copy in first:
+        copy.start()
+    copies = [
+        pltpu.make_async_copy(
+            piece_refs[p].at[pl.ds(start, rows)], hidden.at[pl.ds(to, rows)], sem.at[p]
         )
-    for copy in copies:
+        for p, (to, start, rows) in enumerate(pieces)
+    ]
+    per = GROUP // 128
+    for copy in copies[:per]:
         copy.start()
     core, l_at, y_at = places_ref[16], places_ref[17], places_ref[18]
-    for copy in copies[:4]:
+    for copy in first:
         copy.wait()
+    for copy in copies[per : 2 * per]:
+        copy.start()
+    total = jnp.zeros((16, 512), jnp.float32)
+    for r in range(4):
+        for o in range(2):
+            total += ring[r, o, 256:, :].astype(jnp.float32)
+    for l in range(2):
+        part = jnp.sum(total[:, l * 256 : (l + 1) * 256], axis=1, keepdims=True) * (1 / 64)
+        factor = jnp.minimum(jnp.float32(1.0), jnp.float32(1.0) / jnp.sqrt(part))
+        factors[l] = jnp.broadcast_to(factor, (16, 256))
     halves = [pl.ds(pl.multiple_of(h * 256, 256), 256) for h in (1 - core, core)]
-    for r in range(4):
-        y = (y_at + 4 - r) % 4
-        for o in range(2):
-            l = l_at if o == 0 else 1 - l_at
-            part = (l * 4 + y) * 16
-
-            @pl.loop(0, 16)
-            def _(j):
-                block = places_ref[j]
-                rows = pl.ds(pl.multiple_of(block * 16, 16), 16)
-                to = pl.ds(pl.multiple_of(j * 128 + part, 16), 16)
-                factor = clip_ref[block * 2 + l]
+
+    def assemble(j):
+        block = places_ref[j]
+        rows = pl.ds(pl.multiple_of(block * 16, 16), 16)
+        for r in range(4):
+            y = (y_at + 4 - r) % 4
+            for o in range(2):
+                l = l_at if o == 0 else 1 - l_at
+                to = pl.ds(pl.multiple_of(j * 128 + (l * 4 + y) * 16, 16), 16)
+                factor = factors[l, pl.ds(block, 1), :]
                 for k in range(2):
                     value = ring[r, o, rows, halves[k]].astype(jnp.float32) * factor
                     scaled[to, k * 256 : (k + 1) * 256] = value.astype(jnp.bfloat16)
 
-    for copy in copies[4:]:
-        copy.wait()
     outs = []
-    for i in range(hidden.shape[1] // TILE):
-        at = pl.ds(i * TILE, TILE)
-        acc[:, at] = lax.dot_general(
-            scaled[...], hidden[:, at], (((0,), (0,)), ((), ())), preferred_element_type=jnp.float32
-        )
-        for k, out_ref in enumerate((theirs_ref, mine_ref)):
-            outs.append(
-                pltpu.make_async_copy(
-                    acc.at[pl.ds(k * 256, 256), at], out_ref.at[:, at], out_sem.at[k, i]
+    groups, tiles = hidden.shape[0] // GROUP, hidden.shape[1] // TILE
+    for g in range(groups):
+        depth = pl.ds(g * GROUP, GROUP)
+        for j in range(g * GROUP // 128, (g + 1) * GROUP // 128):
+            assemble(j)
+        for copy in copies[g * per : (g + 1) * per]:
+            copy.wait()
+        for copy in copies[(g + 2) * per : (g + 3) * per]:
+            copy.start()
+        for i in range(tiles):
+            at = pl.ds(i * TILE, TILE)
+            total = lax.dot_general(
+                scaled[depth, :],
+                hidden[depth, at],
+                (((0,), (0,)), ((), ())),
+                preferred_element_type=jnp.float32,
+            )
+            acc[:, at] = total if g == 0 else acc[:, at] + total
+            if g < groups - 1:
+                continue
+            for k, out_ref in enumerate((theirs_ref, mine_ref)):
+                outs.append(
+                    pltpu.make_async_copy(
+                        acc.at[pl.ds(k * 256, 256), at], out_ref.at[:, at], out_sem.at[k, i]
+                    )
                 )
-            )
-            outs[-1].start()
+                outs[-1].start()
     for copy in outs:
         copy.wait()
 
@@ -106,17 +131,18 @@
 COST = pl.CostEstimate(flops=1 << 20, bytes_accessed=1 << 20, transcendentals=0)
 
 
-def product(h, keys, ring, places, clips):
+def product(h, keys, ring, places, tokens):
     tok = 128
     arrays, layout = pieces_of(h, keys, tok)
     ff = arrays[0].shape[1]
     return pl.pallas_call(
-        lambda *refs: product_kernel(layout, *refs),
+        lambda *refs: product_kernel(layout, len(tokens), *refs),
         out_shape=[jax.ShapeDtypeStruct((256, ff), jnp.float32)] * 2,
-        in_specs=[SMEM, SMEM] + [HBM] * (4 + len(arrays)),
+        in_specs=[SMEM] + [HBM] * (4 + len(arrays) + len(tokens)),
         out_specs=[HBM, HBM],
         scratch_shapes=[
             pltpu.VMEM((4,) + ring[0].shape, jnp.bfloat16),
+            pltpu.VMEM((2, 16, 256), jnp.float32),
             pltpu.VMEM((16 * tok, 512), jnp.bfloat16),
             pltpu.VMEM((16 * tok, ff), jnp.bfloat16),
             pltpu.VMEM((512, ff), jnp.float32),
@@ -126,7 +152,7 @@
         ],
         compiler_params=PARAMS,
         cost_estimate=COST,
-    )(places, clips, *ring, *arrays)
+    )(places, *ring, *arrays, *tokens)
 
 
 def split3(value):
@@ -138,6 +164,19 @@
     return parts
 
 
+def weigh(value, flops):
+    def kernel(_, token_ref):
+        token_ref[...] = jnp.zeros_like(token_ref)
+
+    return pl.pallas_call(
+        kernel,
+        out_shape=jax.ShapeDtypeStruct((8, 128), jnp.float32),
+        in_specs=[pl.BlockSpec(memory_space=pl.ANY)],
+        out_specs=VMEM,
+        cost_estimate=pl.CostEstimate(flops=flops, bytes_accessed=1 << 10, transcendentals=0),
+    )(value)
+
+
 def step(inputs, done):
     return lax.optimization_barrier((tuple(inputs), tuple(done)))[0]
 
@@ -178,11 +217,12 @@
     x = ring_x(x)
     h[1, 0], h[0, 2] = [(z, 0, tok)], [(x, 0, tok)]
     message = lax.all_to_all(message, "tensor", 0, 0, tiled=True)
-    x = jnp.concatenate([x, z])
-    z, x, message = step((z, x, message), ())
+    z, x, x2, message, tz0 = step((z, x, z, message, weigh(z, 10737418240)), ())
     z = ring_z(z)
-    x = ring_x(x)
-    h[2, 0], h[0, 3], h[1, 1] = [(z, 0, tok)], [(x, 0, tok)], [(x, tok, tok)]
+    across = ring_x(x)
+    x = ring_x(x2)
+    h[2, 0], h[0, 3], h[1, 1] = [(z, 0, tok)], [(across, 0, tok)], [(x, 0, tok)]
+    message, across = step((message, across), ())
     rows = jnp.sum(message[:, 16:22].astype(jnp.float32).reshape(8, 3, 2048), axis=(0, 1))
     rows = rows.reshape(2, ex, 8 * 64)
     weight_count = jnp.float32(D) * jnp.float32(FF)
@@ -194,16 +234,14 @@
     message = jnp.concatenate([own, jnp.broadcast_to(extra[None], (16, 8, 512))], axis=1)
     groups = [[zx * 2 + c for zx in range(16)] for c in range(2)]
     message = lax.all_to_all(message, "dp", 0, 0, axis_index_groups=groups, tiled=True)
-    across = x[:tok]
-    x = jnp.concatenate([x[tok:], z])
+    x = jnp.concatenate([x, z])
     z, x, across = step((z, x, across), ())
     z = ring_z(z)
     x = ring_x(x)
     h[3, 0], h[1, 2], h[2, 1] = [(z, 0, tok)], [(x, 0, tok)], [(x, tok, tok)]
-    extra = message[:, 16:19].reshape(16, 3, 2, 256)[:, :, :, :64].transpose(0, 2, 1, 3).reshape(16, 384)
-    own = jnp.concatenate(
-        [message[:, :16].reshape(256, 512), jnp.pad(extra, ((0, 0), (0, 128)))]
-    )
+    extra = message[:, 16:19].reshape(16, 3, 2, 256)[:, :, :, :64].transpose(0, 2, 1, 3)
+    extra = jnp.pad(extra, ((0, 0), (0, 0), (0, 1), (0, 0))).reshape(16, 512)
+    own = jnp.concatenate([message[:, :16].reshape(256, 512), extra])
     pair = jnp.stack([own, send(own, zl=1)])
     third = x[:tok]
     x = jnp.concatenate([x[tok:], z])
@@ -213,21 +251,21 @@
     h[3, 3], h[2, 2], h[3, 1] = [(z, 0, tok)], [(x, 0, tok)], [(x, tok, tok)]
     ring = [pair, send(pair, y=1), None, send(pair, y=3)]
     x = jnp.concatenate([x[tok:], third])
-    z, x, pair = step((z, x, pair), (ring[1], ring[3]))
+    z, x, pair, ring[1], ring[3] = step((z, x, pair, ring[1], ring[3]), ())
     z = ring_z(z, -1)
     x = ring_x(x)
     h[2, 3], h[3, 2], h[1, 3] = [(z, 0, tok)], [(x, 0, tok)], [(x, tok, tok)]
     ring[2] = send(pair, y=2)
 
     total = sum(piece[:, 256:].astype(jnp.float32).sum(0) for piece in ring)
-    total = total[:, :384].reshape(16, ex, 3, 64)[:, :, :, 0].sum(2)
+    total = total.reshape(16, ex, 4, 64)[:, :, :, 0].sum(2)
     clips = jnp.minimum(jnp.float32(1.0), jnp.float32(1.0) / jnp.sqrt(total))
     clip_factor = pick(clips, z_at * 4 + x_at)
     keys = [(dz, dx) for dz in range(4) for dx in range(4)]
     way = 1 - 2 * c_at
     places = [((z_at - way * dz) % 4) * 4 + (x_at - way * dx) % 4 for dz, dx in keys]
     places = jnp.stack(places + [c_at, l_at, y_at])
-    theirs, mine = product(h, keys, ring, places, clips.reshape(32))
+    theirs, mine = product(h, keys, ring, places, [tz0])
     total = mine + send(theirs, c=1)
     down_grad = total / jnp.float32(examples) + added_noise.astype(jnp.float32)
     return (down_grad, clip_factor)

time: 138 us -> 126 us (0.913); the launches traced: 138 us -> 124 us
  starting transfers between devices: 52.2 us -> 42.5 us
  waiting for transfers between devices: 54.6 us -> 51.9 us
    ppermute x16 -> x17, starting transfers between devices: 38.1 us -> 32.6 us  [permute(): return lax.ppermute(value, ('dp', 'tensor'), pairs)]
    ppermute x16 -> x17, waiting for transfers between devices: 47.6 us -> 42.5 us  [permute(): return lax.ppermute(value, ('dp', 'tensor'), pairs)]
    all_to_all x1, waiting for transfers between devices: 0.01 us -> 3.88 us  [per_device(): lax.all_to_all(message, 'dp', 0, 0, axis_index_groups=groups, tiled=True)]
    all_to_all x1, starting transfers between devices: 8.56 us -> 5.23 us  [per_device(): lax.all_to_all(message, 'dp', 0, 0, axis_index_groups=groups, tiled=True)]
    all_to_all x1, waiting for transfers between devices: 7.01 us -> 5.53 us  [per_device(): message = lax.all_to_all(message, 'tensor', 0, 0, tiled=True)]
    unnamed x34 -> x39, local copies, waits for them, and re-layouts: 2.73 us -> 3.77 us
    pallas_call x1 -> x2, Pallas kernels: 11.4 us -> 10.4 us  [the longest x1 9.8 us: product(): pl.pallas_call(lambda *refs: product_kernel(layout, len(tokens), *refs),...]
  transfers between devices with their start and end apart: 18 -> 19, of which waited for: 8 -> 12; matrix products, arithmetic and copies ran while one was open for 8% -> 8% of each run, Pallas kernels for 0% -> 0%
where the time goes in v2:
time: 126 us; the launch traced here: 124 us
  waiting for transfers between devices  51.9 us (41%)
  starting transfers between devices  42.5 us (34%)
  Pallas kernels  10.4 us (8%)
  other arithmetic  10.3 us (8%)
  local copies, waits for them, and re-layouts  7.48 us (6%)
    ppermute x17, waiting for transfers between devices, permute(): return lax.ppermute(value, ('dp', 'tensor'), pairs)  42.5 us
    ppermute x17, starting transfers between devices, permute(): return lax.ppermute(value, ('dp', 'tensor'), pairs)  32.6 us
    pallas_call x1, Pallas kernels, product(): pl.pallas_call(lambda *refs: product_kernel(layout, len(tokens), *refs),...  9.8 us
    all_to_all x1, waiting for transfers between devices, per_device(): message = lax.all_to_all(message, 'tensor', 0, 0, tiled=True)  5.53 us
    all_to_all x1, starting transfers between devices, per_device(): lax.all_to_all(message, 'dp', 0, 0, axis_index_groups=groups, tiled=True)  5.23 us
    all_to_all x1, starting transfers between devices, per_device(): message = lax.all_to_all(message, 'tensor', 0, 0, tiled=True)  4.66 us
    all_to_all x1, waiting for transfers between devices, per_device(): lax.all_to_all(message, 'dp', 0, 0, axis_index_groups=groups, tiled=True)  3.88 us
    unnamed x39, local copies, waits for them, and re-layouts  3.77 us
  transfers between devices with their start and end apart: 19, of which 12 were waited for; matrix products, arithmetic and copies ran while one was open for 8% of the time, Pallas kernels for 0%

profile of v2, /device:TPU:1, one launch (start us, length us, event | category | flops | bytes accessed | tf_op | source)
XLA Modules:
  0.0 124.0 jit_solution(11228602391147330276)
XLA Ops:
  0.6 1.5 %fusion.4.refs_5_ = bf16[128,1792]{1,0:T(8,128)(2,1)S(1)} fusion(bf16[128,1792]{1,0:T(8,128)(2,1)} %param.6, bf16[128,1792]{1,0:T(8,128)(2,1)} %param.5), kind=kLoop, calls=%fused_computation.12 | loop fusion | flops 1835008 | bytes 1376256 | tf_op jit(solution)/shard_map/convert_element_type | solution.py:197
  2.1 3.4 %collective-permute-start.1 = (bf16[128,1792]{1,0:T(8,128)(2,1)S(1)}, bf16[128,1792]{1,0:T(8,128)(2,1)S(1)}, u32[]{:S(2)}, u32[]{:S(2)}) collective-permute-start(bf16[128,1792]{1,0:T(8,128)(2,1)S(1)} %fusion.4.refs_5_), channel_id=1, source_target_pairs={{0,16},{1,17},{2,18},{3,19},{4,20},{5,21},{6,22},{7,23},{8,56},{9,... | collective-permute-start | bytes 1376264 | tf_op jit(solution)/shard_map/ppermute | solution.py:29
  5.5 6.0 %collective-permute-start = (bf16[128,1792]{1,0:T(8,128)(2,1)S(1)}, bf16[128,1792]{1,0:T(8,128)(2,1)S(1)}, u32[]{:S(2)}, u32[]{:S(2)}) collective-permute-start(bf16[128,1792]{1,0:T(8,128)(2,1)S(1)} %fusion.4.refs_5_), channel_id=1, source_target_pairs={{0,64},{1,65},{2,66},{3,67},{4,68},{5,69},{6,70},{7,71},{8,200},{9... | collective-permute-start | bytes 1376264 | tf_op jit(solution)/shard_map/ppermute | solution.py:29
  12.3 1.6 %concatenate.25 = bf16[8,24,1024]{2,1,0:T(8,128)(2,1)} concatenate(bf16[8,16,1024]{2,1,0:T(8,128)(2,1)S(1)} %bitcast.50, bf16[8,2,1024]{2,1,0:T(2,128)(2,1)S(1)} %copy.19, bf16[8,2,1024]{2,1,0:T(2,128)(2,1)S(1)} %copy.20, bf16[8,2,1024]{2,1,0:T(2,128)(2,1)S(1)} %copy.21, bf16[8,2,1024]{2,1,0:T(2,128)(2,1)S(1)} %broadcast_in_dim.15), dimensions={1} | concatenate | bytes 786432 | tf_op jit(solution)/shard_map/concatenate | solution.py:209
  13.9 4.7 %all-to-all-start = ((bf16[8,24,1024]{2,1,0:T(8,128)(2,1)}), bf16[8,24,1024]{2,1,0:T(8,128)(2,1)S(1)}, u32[]{:S(2)}, u32[]{:S(2)}) async-start(bf16[8,24,1024]{2,1,0:T(8,128)(2,1)} %concatenate.25), calls=%async_computation | async-start | bytes 786432 | tf_op jit(solution)/shard_map/all_to_all | solution.py:219
  19.2 1.7 %collective-permute-done._.refs_9_ = bf16[128,1792]{1,0:T(8,128)(2,1)S(1)} collective-permute-done((bf16[128,1792]{1,0:T(8,128)(2,1)S(1)}, bf16[128,1792]{1,0:T(8,128)(2,1)S(1)}, u32[]{:S(2)}, u32[]{:S(2)}) %collective-permute-start) | collective-permute-done | bytes 458784 | tf_op jit(solution)/shard_map/ppermute | solution.py:29
  21.0 0.8 copy-done.13
  22.4 5.5 %all-to-all-done = bf16[8,24,1024]{2,1,0:T(8,128)(2,1)S(1)} async-done(((bf16[8,24,1024]{2,1,0:T(8,128)(2,1)}), bf16[8,24,1024]{2,1,0:T(8,128)(2,1)S(1)}, u32[]{:S(2)}, u32[]{:S(2)}) %all-to-all-start) | async-done | bytes 393248 | tf_op jit(solution)/shard_map/all_to_all | solution.py:219
  28.5 2.6 %collective-permute-start.3 = (bf16[128,1792]{1,0:T(8,128)(2,1)}, bf16[128,1792]{1,0:T(8,128)(2,1)S(1)}, u32[]{:S(2)}, u32[]{:S(2)}) collective-permute-start(bf16[128,1792]{1,0:T(8,128)(2,1)} %copy-done.13), channel_id=1, source_target_pairs={{0,64},{1,65},{2,66},{3,67},{4,68},{5,69},{6,70},{7,71},{8,200},{9... | collective-permute-start | bytes 1376264 | tf_op jit(solution)/shard_map/ppermute | solution.py:29
  31.1 4.4 %collective-permute-done.5.refs_8_ = bf16[128,1792]{1,0:T(8,128)(2,1)S(1)} collective-permute-done((bf16[128,1792]{1,0:T(8,128)(2,1)S(1)}, bf16[128,1792]{1,0:T(8,128)(2,1)S(1)}, u32[]{:S(2)}, u32[]{:S(2)}) %collective-permute-start.5) | collective-permute-done | bytes 458784 | tf_op jit(solution)/shard_map/ppermute | solution.py:29
  37.6 5.2 %all-to-all-start.1 = ((bf16[16,24,512]{2,1,0:T(8,128)(2,1)}), bf16[16,24,512]{2,1,0:T(8,128)(2,1)S(1)}, u32[]{:S(2)}, u32[]{:S(2)}) async-start(bf16[16,24,512]{2,1,0:T(8,128)(2,1)} %pad_maximum_fusion.4), calls=%async_computation.1 | async-start | bytes 786432 | tf_op jit(solution)/shard_map/all_to_all | solution.py:236
  42.9 1.1 pad_maximum_fusion
  44.0 2.6 %collective-permute-start.6 = (bf16[256,1792]{1,0:T(8,128)(2,1)}, bf16[256,1792]{1,0:T(8,128)(2,1)S(1)}, u32[]{:S(2)}, u32[]{:S(2)}) collective-permute-start(bf16[256,1792]{1,0:T(8,128)(2,1)} %pad_maximum_fusion), channel_id=1, source_target_pairs={{0,16},{1,17},{2,18},{3,19},{4,20},{5,21},{6,22},{7,23},{8,56},{9,... | collective-permute-start | bytes 2752520 | tf_op jit(solution)/shard_map/ppermute | solution.py:29
  46.5 3.3 %collective-permute-start.7 = (bf16[128,1792]{1,0:T(8,128)(2,1)S(1)}, bf16[128,1792]{1,0:T(8,128)(2,1)S(1)}, u32[]{:S(2)}, u32[]{:S(2)}) collective-permute-start(bf16[128,1792]{1,0:T(8,128)(2,1)S(1)} %collective-permute-done.3.refs_13_), channel_id=1, source_target_pairs={{0,64},{1,65},{2,66},{3,67},{4,68},{5,69},{6,70},{7,71},{8,200},{9... | collective-permute-start | bytes 1376264 | tf_op jit(solution)/shard_map/ppermute | solution.py:29
  49.8 3.9 %all-to-all-done.1 = bf16[16,24,512]{2,1,0:T(8,128)(2,1)S(1)} async-done(((bf16[16,24,512]{2,1,0:T(8,128)(2,1)}), bf16[16,24,512]{2,1,0:T(8,128)(2,1)S(1)}, u32[]{:S(2)}, u32[]{:S(2)}) %all-to-all-start.1) | async-done | bytes 393248 | tf_op jit(solution)/shard_map/all_to_all | solution.py:236
  54.0 2.2 %collective-permute-start.8 = (bf16[272,512]{1,0:T(8,128)(2,1)S(1)}, bf16[272,512]{1,0:T(8,128)(2,1)S(1)}, u32[]{:S(2)}, u32[]{:S(2)}) collective-permute-start(bf16[272,512]{1,0:T(8,128)(2,1)S(1)} %get-tuple-element.47), channel_id=1, source_target_pairs={{0,4},{1,5},{2,6},{3,7},{4,0},{5,1},{6,2},{7,3},{8,12},{9,13},{10,... | collective-permute-start | bytes 835592 | tf_op jit(solution)/shard_map/ppermute | solution.py:29
  56.2 4.3 %collective-permute-done.6.refs_11_.refs_14_ = bf16[256,1792]{1,0:T(8,128)(2,1)S(1)} collective-permute-done((bf16[256,1792]{1,0:T(8,128)(2,1)}, bf16[256,1792]{1,0:T(8,128)(2,1)S(1)}, u32[]{:S(2)}, u32[]{:S(2)}) %collective-permute-start.6) | collective-permute-done | bytes 917536 | tf_op jit(solution)/shard_map/ppermute | solution.py:29
  60.5 4.4 %collective-permute-done.7.refs_17_ = bf16[128,1792]{1,0:T(8,128)(2,1)S(1)} collective-permute-done((bf16[128,1792]{1,0:T(8,128)(2,1)S(1)}, bf16[128,1792]{1,0:T(8,128)(2,1)S(1)}, u32[]{:S(2)}, u32[]{:S(2)}) %collective-permute-start.7) | collective-permute-done | bytes 458784 | tf_op jit(solution)/shard_map/ppermute | solution.py:29
  65.0 2.7 %collective-permute-done.8 = bf16[272,512]{1,0:T(8,128)(2,1)S(1)} collective-permute-done((bf16[272,512]{1,0:T(8,128)(2,1)S(1)}, bf16[272,512]{1,0:T(8,128)(2,1)S(1)}, u32[]{:S(2)}, u32[]{:S(2)}) %collective-permute-start.8) | collective-permute-done | bytes 278560 | tf_op jit(solution)/shard_map/ppermute | solution.py:29
  67.8 3.6 %collective-permute-start.10 = (bf16[256,1792]{1,0:T(8,128)(2,1)S(1)}, bf16[256,1792]{1,0:T(8,128)(2,1)S(1)}, u32[]{:S(2)}, u32[]{:S(2)}) collective-permute-start(bf16[256,1792]{1,0:T(8,128)(2,1)S(1)} %pad_maximum_fusion.1), channel_id=1, source_target_pairs={{0,16},{1,17},{2,18},{3,19},{4,20},{5,21},{6,22},{7,23},{8,56},{9,... | collective-permute-start | bytes 2752520 | tf_op jit(solution)/shard_map/ppermute | solution.py:29
  71.8 1.1 collective-permute-start.11
  72.9 0.9 collective-permute-start.9
  73.8 8.0 %collective-permute-done.10.refs_15_.refs_18_ = bf16[256,1792]{1,0:T(8,128)(2,1)S(1)} collective-permute-done((bf16[256,1792]{1,0:T(8,128)(2,1)S(1)}, bf16[256,1792]{1,0:T(8,128)(2,1)S(1)}, u32[]{:S(2)}, u32[]{:S(2)}) %collective-permute-start.10) | collective-permute-done | bytes 917536 | tf_op jit(solution)/shard_map/ppermute | solution.py:29
  81.8 1.1 pad_maximum_fusion.2
  82.9 4.3 %collective-permute-done.9.refs_20_ = bf16[128,1792]{1,0:T(8,128)(2,1)} collective-permute-done((bf16[128,1792]{1,0:T(8,128)(2,1)S(1)}, bf16[128,1792]{1,0:T(8,128)(2,1)}, u32[]{:S(2)}, u32[]{:S(2)}) %collective-permute-start.9) | collective-permute-done | bytes 458784 | tf_op jit(solution)/shard_map/ppermute | solution.py:29
  87.1 0.8 copy-done.10
  88.8 1.1 collective-permute-start.13
  90.7 11.7 %collective-permute-done.15.refs_16_ = bf16[128,1792]{1,0:T(8,128)(2,1)} collective-permute-done((bf16[128,1792]{1,0:T(8,128)(2,1)}, bf16[128,1792]{1,0:T(8,128)(2,1)}, u32[]{:S(2)}, u32[]{:S(2)}) %collective-permute-start.15) | collective-permute-done | bytes 458784 | tf_op jit(solution)/shard_map/ppermute | solution.py:29
  103.1 0.9 copy-done.3
  104.0 9.8 %shard_map.69 = (f32[256,1792]{1,0:T(8,128)}, f32[256,1792]{1,0:T(8,128)}) custom-call(s32[19]{0:T(128)} %stack.97.refs_0_, bf16[2,272,512]{2,1,0:T(8,128)(2,1)} %copy-done.4, bf16[2,272,512]{2,1,0:T(8,128)(2,1)} %copy-done.11, bf16[2,272,512]{2,1,0:T(8,128)(2,1)} %collective-permute-done.13.refs_3_, bf16[2,272,512]{2,1,0:T(8,128)(2,1)} %copy-done.10, ...), custom_call_target="tpu_custom_call" | custom-call | flops 1048576 | bytes 1048576 | tf_op jit(solution)/shard_map/pallas_call | solution.py:138
  113.8 3.6 %collective-permute-start.16 = (f32[256,1792]{1,0:T(8,128)}, f32[256,1792]{1,0:T(8,128)S(1)}, u32[]{:S(2)}, u32[]{:S(2)}) collective-permute-start(f32[256,1792]{1,0:T(8,128)} %get-tuple-element.41), channel_id=1, source_target_pairs={{0,8},{1,9},{2,10},{3,11},{4,12},{5,13},{6,14},{7,15},{8,0},{9,1},... | collective-permute-start | bytes 5505032 | tf_op jit(solution)/shard_map/ppermute | solution.py:29
  121.0 3.0 %convert_add_fusion = f32[256,1792]{1,0:T(8,128)} fusion(bf16[256,1792]{1,0:T(8,128)(2,1)S(1)} %copy-done.9, f32[256,1792]{1,0:T(8,128)} %get-tuple-element.40, f32[256,1792]{1,0:T(8,128)S(1)} %collective-permute-done.16), kind=kLoop, calls=%fused_computation | loop fusion | flops 1835008 | bytes 6422528 | tf_op jit(solution)/shard_map/add | solution.py:270
  (95 shorter events, 11.3 us)
Async XLA Ops:
  0.6 11.2 %copy-start.5 = (bf16[128,1024]{1,0:T(8,128)(2,1)S(1)}, bf16[128,1024]{1,0:T(8,128)(2,1)}, u32[]{:S(2)}) copy-start(bf16[128,1024]{1,0:T(8,128)(2,1)} %param.7) | copy-start | bytes 786436
  2.1 11.8 %copy-start.1 = (bf16[128,1792]{1,0:T(8,128)(2,1)}, bf16[128,1792]{1,0:T(8,128)(2,1)S(1)}, u32[]{:S(2)}) copy-start(bf16[128,1792]{1,0:T(8,128)(2,1)S(1)} %fusion.4.refs_5_) | copy-start | bytes 1376260
  2.1 16.5 %collective-permute-start.1 = (bf16[128,1792]{1,0:T(8,128)(2,1)S(1)}, bf16[128,1792]{1,0:T(8,128)(2,1)S(1)}, u32[]{:S(2)}, u32[]{:S(2)}) collective-permute-start(bf16[128,1792]{1,0:T(8,128)(2,1)S(1)} %fusion.4.refs_5_), channel_id=1, source_target_pairs={{0,16},{1,17},{2,18},{3,19},{4,20},{5,21},{6,22},{7,23},{8,56},{9,... | collective-permute-start | bytes 1376264 | tf_op jit(solution)/shard_map/ppermute | solution.py:29
  5.5 15.4 %collective-permute-start = (bf16[128,1792]{1,0:T(8,128)(2,1)S(1)}, bf16[128,1792]{1,0:T(8,128)(2,1)S(1)}, u32[]{:S(2)}, u32[]{:S(2)}) collective-permute-start(bf16[128,1792]{1,0:T(8,128)(2,1)S(1)} %fusion.4.refs_5_), channel_id=1, source_target_pairs={{0,64},{1,65},{2,66},{3,67},{4,68},{5,69},{6,70},{7,71},{8,200},{9... | collective-permute-start | bytes 1376264 | tf_op jit(solution)/shard_map/ppermute | solution.py:29
  13.9 14.0 %all-to-all-start = ((bf16[8,24,1024]{2,1,0:T(8,128)(2,1)}), bf16[8,24,1024]{2,1,0:T(8,128)(2,1)S(1)}, u32[]{:S(2)}, u32[]{:S(2)}) async-start(bf16[8,24,1024]{2,1,0:T(8,128)(2,1)} %concatenate.25), calls=%async_computation | async-start | bytes 786432 | tf_op jit(solution)/shard_map/all_to_all | solution.py:219
  18.6 18.0 %copy-start.17 = (f32[2]{0:T(128)S(1)}, f32[2]{0:T(128)}, u32[]{:S(2)}) copy-start(f32[2]{0:T(128)} %param.8) | copy-start | bytes 28
  18.6 3.8 %copy-start.12 = (bf16[128,1792]{1,0:T(8,128)(2,1)}, bf16[128,1792]{1,0:T(8,128)(2,1)S(1)}, u32[]{:S(2)}) copy-start(bf16[128,1792]{1,0:T(8,128)(2,1)S(1)} %collective-permute-done.1.refs_6_) | copy-start | bytes 1376260
  18.6 9.3 %collective-permute-start.2 = (bf16[128,1792]{1,0:T(8,128)(2,1)S(1)}, bf16[128,1792]{1,0:T(8,128)(2,1)S(1)}, u32[]{:S(2)}, u32[]{:S(2)}) collective-permute-start(bf16[128,1792]{1,0:T(8,128)(2,1)S(1)} %collective-permute-done.1.refs_6_), channel_id=1, source_target_pairs={{0,16},{1,17},{2,18},{3,19},{4,20},{5,21},{6,22},{7,23},{8,56},{9,... | collective-permute-start | bytes 1376264 | tf_op jit(solution)/shard_map/ppermute | solution.py:29
  27.9 9.7 %copy-start.14 = (bf16[128,1792]{1,0:T(8,128)(2,1)}, bf16[128,1792]{1,0:T(8,128)(2,1)S(1)}, u32[]{:S(2)}) copy-start(bf16[128,1792]{1,0:T(8,128)(2,1)S(1)} %collective-permute-done.2.refs_7_) | copy-start | bytes 1376260
  27.9 7.6 %collective-permute-start.5 = (bf16[128,1792]{1,0:T(8,128)(2,1)S(1)}, bf16[128,1792]{1,0:T(8,128)(2,1)S(1)}, u32[]{:S(2)}, u32[]{:S(2)}) collective-permute-start(bf16[128,1792]{1,0:T(8,128)(2,1)S(1)} %collective-permute-done.2.refs_7_), channel_id=1, source_target_pairs={{0,16},{1,17},{2,18},{3,19},{4,20},{5,21},{6,22},{7,23},{8,56},{9,... | collective-permute-start | bytes 1376264 | tf_op jit(solution)/shard_map/ppermute | solution.py:29
  28.5 14.3 %collective-permute-start.3 = (bf16[128,1792]{1,0:T(8,128)(2,1)}, bf16[128,1792]{1,0:T(8,128)(2,1)S(1)}, u32[]{:S(2)}, u32[]{:S(2)}) collective-permute-start(bf16[128,1792]{1,0:T(8,128)(2,1)} %copy-done.13), channel_id=1, source_target_pairs={{0,64},{1,65},{2,66},{3,67},{4,68},{5,69},{6,70},{7,71},{8,200},{9... | collective-permute-start | bytes 1376264 | tf_op jit(solution)/shard_map/ppermute | solution.py:29
  31.1 11.8 %collective-permute-start.4 = (bf16[128,1792]{1,0:T(8,128)(2,1)}, bf16[128,1792]{1,0:T(8,128)(2,1)S(1)}, u32[]{:S(2)}, u32[]{:S(2)}) collective-permute-start(bf16[128,1792]{1,0:T(8,128)(2,1)} %copy-done.13), channel_id=1, source_target_pairs={{0,16},{1,17},{2,18},{3,19},{4,20},{5,21},{6,22},{7,23},{8,56},{9,... | collective-permute-start | bytes 1376264 | tf_op jit(solution)/shard_map/ppermute | solution.py:29
  37.6 16.1 %all-to-all-start.1 = ((bf16[16,24,512]{2,1,0:T(8,128)(2,1)}), bf16[16,24,512]{2,1,0:T(8,128)(2,1)S(1)}, u32[]{:S(2)}, u32[]{:S(2)}) async-start(bf16[16,24,512]{2,1,0:T(8,128)(2,1)} %pad_maximum_fusion.4), calls=%async_computation.1 | async-start | bytes 786432 | tf_op jit(solution)/shard_map/all_to_all | solution.py:236
  42.9 17.6 %copy-start.6 = (bf16[128,1792]{1,0:T(8,128)(2,1)}, bf16[128,1792]{1,0:T(8,128)(2,1)S(1)}, u32[]{:S(2)}) copy-start(bf16[128,1792]{1,0:T(8,128)(2,1)S(1)} %collective-permute-done.3.refs_13_) | copy-start | bytes 1376260
  42.9 17.6 %copy-start.7 = (bf16[128,1792]{1,0:T(8,128)(2,1)}, bf16[128,1792]{1,0:T(8,128)(2,1)S(1)}, u32[]{:S(2)}) copy-start(bf16[128,1792]{1,0:T(8,128)(2,1)S(1)} %collective-permute-done.4.refs_10_) | copy-start | bytes 1376260
  44.0 16.4 %collective-permute-start.6 = (bf16[256,1792]{1,0:T(8,128)(2,1)}, bf16[256,1792]{1,0:T(8,128)(2,1)S(1)}, u32[]{:S(2)}, u32[]{:S(2)}) collective-permute-start(bf16[256,1792]{1,0:T(8,128)(2,1)} %pad_maximum_fusion), channel_id=1, source_target_pairs={{0,16},{1,17},{2,18},{3,19},{4,20},{5,21},{6,22},{7,23},{8,56},{9,... | collective-permute-start | bytes 2752520 | tf_op jit(solution)/shard_map/ppermute | solution.py:29
  46.5 18.4 %collective-permute-start.7 = (bf16[128,1792]{1,0:T(8,128)(2,1)S(1)}, bf16[128,1792]{1,0:T(8,128)(2,1)S(1)}, u32[]{:S(2)}, u32[]{:S(2)}) collective-permute-start(bf16[128,1792]{1,0:T(8,128)(2,1)S(1)} %collective-permute-done.3.refs_13_), channel_id=1, source_target_pairs={{0,64},{1,65},{2,66},{3,67},{4,68},{5,69},{6,70},{7,71},{8,200},{9... | collective-permute-start | bytes 1376264 | tf_op jit(solution)/shard_map/ppermute | solution.py:29
  54.0 13.7 %collective-permute-start.8 = (bf16[272,512]{1,0:T(8,128)(2,1)S(1)}, bf16[272,512]{1,0:T(8,128)(2,1)S(1)}, u32[]{:S(2)}, u32[]{:S(2)}) collective-permute-start(bf16[272,512]{1,0:T(8,128)(2,1)S(1)} %get-tuple-element.47), channel_id=1, source_target_pairs={{0,4},{1,5},{2,6},{3,7},{4,0},{5,1},{6,2},{7,3},{8,12},{9,13},{10,... | collective-permute-start | bytes 835592 | tf_op jit(solution)/shard_map/ppermute | solution.py:29
  60.4 4.6 %copy-start = (bf16[256,1792]{1,0:T(8,128)(2,1)}, bf16[256,1792]{1,0:T(8,128)(2,1)S(1)}, u32[]{:S(2)}) copy-start(bf16[256,1792]{1,0:T(8,128)(2,1)S(1)} %collective-permute-done.6.refs_11_.refs_14_) | copy-start | bytes 2752516
  60.5 12.4 %copy-start.16 = (bf16[128,1792]{1,0:T(8,128)(2,1)S(1)}, bf16[128,1792]{1,0:T(8,128)(2,1)}, u32[]{:S(2)}) copy-start(bf16[128,1792]{1,0:T(8,128)(2,1)} %copy-done.15) | copy-start | bytes 1376260
  64.9 8.8 %copy-start.8 = (bf16[128,1792]{1,0:T(8,128)(2,1)}, bf16[128,1792]{1,0:T(8,128)(2,1)S(1)}, u32[]{:S(2)}) copy-start(bf16[128,1792]{1,0:T(8,128)(2,1)S(1)} %collective-permute-done.7.refs_17_) | copy-start | bytes 1376260
  67.8 35.3 %copy-start.4 = (bf16[2,272,512]{2,1,0:T(8,128)(2,1)}, bf16[2,272,512]{2,1,0:T(8,128)(2,1)S(1)}, u32[]{:S(2)}) copy-start(bf16[2,272,512]{2,1,0:T(8,128)(2,1)S(1)} %pad_maximum_fusion.3.refs_1_) | copy-start | bytes 1671172
  67.8 14.0 %collective-permute-start.10 = (bf16[256,1792]{1,0:T(8,128)(2,1)S(1)}, bf16[256,1792]{1,0:T(8,128)(2,1)S(1)}, u32[]{:S(2)}, u32[]{:S(2)}) collective-permute-start(bf16[256,1792]{1,0:T(8,128)(2,1)S(1)} %pad_maximum_fusion.1), channel_id=1, source_target_pairs={{0,16},{1,17},{2,18},{3,19},{4,20},{5,21},{6,22},{7,23},{8,56},{9,... | collective-permute-start | bytes 2752520 | tf_op jit(solution)/shard_map/ppermute | solution.py:29
  71.4 15.7 %collective-permute-start.12 = (bf16[2,272,512]{2,1,0:T(8,128)(2,1)S(1)}, bf16[2,272,512]{2,1,0:T(8,128)(2,1)S(1)}, u32[]{:S(2)}, u32[]{:S(2)}) collective-permute-start(bf16[2,272,512]{2,1,0:T(8,128)(2,1)S(1)} %pad_maximum_fusion.3.refs_1_), channel_id=1, source_target_pairs={{0,3},{1,0},{2,1},{3,2},{4,7},{5,4},{6,5},{7,6},{8,11},{9,8},{10,9... | collective-permute-start | bytes 1671176 | tf_op jit(solution)/shard_map/ppermute | solution.py:29
  71.8 15.4 %collective-permute-start.11 = (bf16[2,272,512]{2,1,0:T(8,128)(2,1)S(1)}, bf16[2,272,512]{2,1,0:T(8,128)(2,1)S(1)}, u32[]{:S(2)}, u32[]{:S(2)}) collective-permute-start(bf16[2,272,512]{2,1,0:T(8,128)(2,1)S(1)} %pad_maximum_fusion.3.refs_1_), channel_id=1, source_target_pairs={{0,1},{1,2},{2,3},{3,0},{4,5},{5,6},{6,7},{7,4},{8,9},{9,10},{10,1... | collective-permute-start | bytes 1671176 | tf_op jit(solution)/shard_map/ppermute | solution.py:29
  72.9 14.3 %collective-permute-start.9 = (bf16[128,1792]{1,0:T(8,128)(2,1)S(1)}, bf16[128,1792]{1,0:T(8,128)(2,1)}, u32[]{:S(2)}, u32[]{:S(2)}) collective-permute-start(bf16[128,1792]{1,0:T(8,128)(2,1)S(1)} %copy-done.16), channel_id=1, source_target_pairs={{0,192},{1,193},{2,194},{3,195},{4,196},{5,197},{6,198},{7,199},{8... | collective-permute-start | bytes 1376264 | tf_op jit(solution)/shard_map/ppermute | solution.py:29
  81.7 21.3 %copy-start.2 = (bf16[256,1792]{1,0:T(8,128)(2,1)}, bf16[256,1792]{1,0:T(8,128)(2,1)S(1)}, u32[]{:S(2)}) copy-start(bf16[256,1792]{1,0:T(8,128)(2,1)S(1)} %collective-permute-done.10.refs_15_.refs_18_) | copy-start | bytes 2752516
  87.9 15.1 %collective-permute-start.14 = (bf16[256,1792]{1,0:T(8,128)(2,1)}, bf16[256,1792]{1,0:T(8,128)(2,1)S(1)}, u32[]{:S(2)}, u32[]{:S(2)}) collective-permute-start(bf16[256,1792]{1,0:T(8,128)(2,1)} %pad_maximum_fusion.2), channel_id=1, source_target_pairs={{0,16},{1,17},{2,18},{3,19},{4,20},{5,21},{6,22},{7,23},{8,56},{9,... | collective-permute-start | bytes 2752520 | tf_op jit(solution)/shard_map/ppermute | solution.py:29
  88.8 14.3 %collective-permute-start.13 = (bf16[2,272,512]{2,1,0:T(8,128)(2,1)S(1)}, bf16[2,272,512]{2,1,0:T(8,128)(2,1)}, u32[]{:S(2)}, u32[]{:S(2)}) collective-permute-start(bf16[2,272,512]{2,1,0:T(8,128)(2,1)S(1)} %pad_maximum_fusion.3.refs_1_), channel_id=1, source_target_pairs={{0,2},{1,3},{2,0},{3,1},{4,6},{5,7},{6,4},{7,5},{8,10},{9,11},{10,... | collective-permute-start | bytes 1671176 | tf_op jit(solution)/shard_map/ppermute | solution.py:29
  89.9 12.5 %collective-permute-start.15 = (bf16[128,1792]{1,0:T(8,128)(2,1)}, bf16[128,1792]{1,0:T(8,128)(2,1)}, u32[]{:S(2)}, u32[]{:S(2)}) collective-permute-start(bf16[128,1792]{1,0:T(8,128)(2,1)} %collective-permute-done.9.refs_20_), channel_id=1, source_target_pairs={{0,192},{1,193},{2,194},{3,195},{4,196},{5,197},{6,198},{7,199},{8... | collective-permute-start | bytes 1376264 | tf_op jit(solution)/shard_map/ppermute | solution.py:29
  90.7 30.4 %copy-start.9 = (bf16[256,1792]{1,0:T(8,128)(2,1)S(1)}, bf16[256,1792]{1,0:T(8,128)(2,1)}, u32[]{:S(2)}) copy-start(bf16[256,1792]{1,0:T(8,128)(2,1)} %param.9) | copy-start | bytes 2752516
  113.8 7.2 %collective-permute-start.16 = (f32[256,1792]{1,0:T(8,128)}, f32[256,1792]{1,0:T(8,128)S(1)}, u32[]{:S(2)}, u32[]{:S(2)}) collective-permute-start(f32[256,1792]{1,0:T(8,128)} %get-tuple-element.41), channel_id=1, source_target_pairs={{0,8},{1,9},{2,10},{3,11},{4,12},{5,13},{6,14},{7,15},{8,0},{9,1},... | collective-permute-start | bytes 5505032 | tf_op jit(solution)/shard_map/ppermute | solution.py:29
  (5 other events, 4.2 us)

commit v3 on v2

--- a/solution.py
+++ b/solution.py
@@ -206,9 +206,9 @@
         ]
     )
     rows = grams.reshape(2, ex, 8, 8, 64).transpose(2, 0, 1, 3, 4).reshape(8, 2, 1024)
-    message = jnp.concatenate(
-        [out_grad.reshape(8, 16, 1024)] + split3(rows) + [jnp.zeros((8, 2, 1024), jnp.bfloat16)], axis=1
-    )
+    rows = jnp.concatenate(split3(rows) + [jnp.zeros((8, 2, 1024), jnp.bfloat16)], axis=1)
+    rows = step((rows,), ())[0]
+    message = jnp.concatenate([out_grad.reshape(8, 16, 1024), rows], axis=1)
 
     h = {(0, 0): [(hidden, 0, tok)]}
     z = ring_z(hidden)
@@ -255,6 +255,7 @@
     z = ring_z(z, -1)
     x = ring_x(x)
     h[2, 3], h[3, 2], h[1, 3] = [(z, 0, tok)], [(x, 0, tok)], [(x, tok, tok)]
+    tz4 = weigh(z, 3 << 30)
     ring[2] = send(pair, y=2)
 
     total = sum(piece[:, 256:].astype(jnp.float32).sum(0) for piece in ring)
@@ -265,7 +266,7 @@
     way = 1 - 2 * c_at
     places = [((z_at - way * dz) % 4) * 4 + (x_at - way * dx) % 4 for dz, dx in keys]
     places = jnp.stack(places + [c_at, l_at, y_at])
-    theirs, mine = product(h, keys, ring, places, [tz0])
+    theirs, mine = product(h, keys, ring, places, [tz0, tz4])
     total = mine + send(theirs, c=1)
     down_grad = total / jnp.float32(examples) + added_noise.astype(jnp.float32)
     return (down_grad, clip_factor)

time: 126 us -> 123 us (0.976); the launches traced: 124 us -> 122 us
  local copies, waits for them, and re-layouts: 7.48 us -> 4.87 us
  waiting for transfers between devices: 51.9 us -> 49.4 us
    ppermute x17, waiting for transfers between devices: 42.5 us -> 40.3 us  [permute(): return lax.ppermute(value, ('dp', 'tensor'), pairs)]
    concatenate x1, local copies, waits for them, and re-layouts: 1.6 us -> 0.08 us  [per_device(): jnp.concatenate(split3(rows) + [jnp.zeros((8, 2, 1024), jnp.bfloat16)], a...]
    unnamed x39 -> x43, local copies, waits for them, and re-layouts: 3.77 us -> 2.72 us
  transfers between devices with their start and end apart: 19 -> 19, of which waited for: 12 -> 11; matrix products, arithmetic and copies ran while one was open for 8% -> 9% of each run, Pallas kernels for 0% -> 1%
where the time goes in v3:
time: 123 us; the launch traced here: 122 us
  waiting for transfers between devices  49.4 us (40%)
  starting transfers between devices  43.5 us (35%)
  other arithmetic  11.3 us (9%)
  Pallas kernels  10.8 us (9%)
  local copies, waits for them, and re-layouts  4.87 us (4%)
  matrix products  1.48 us (1%)
    ppermute x17, waiting for transfers between devices, permute(): return lax.ppermute(value, ('dp', 'tensor'), pairs)  40.3 us
    ppermute x17, starting transfers between devices, permute(): return lax.ppermute(value, ('dp', 'tensor'), pairs)  33.6 us
    pallas_call x1, Pallas kernels, product(): pl.pallas_call(lambda *refs: product_kernel(layout, len(tokens), *refs),...  9.65 us
    all_to_all x1, waiting for transfers between devices, per_device(): message = lax.all_to_all(message, 'tensor', 0, 0, tiled=True)  5.24 us
    all_to_all x1, starting transfers between devices, per_device(): lax.all_to_all(message, 'dp', 0, 0, axis_index_groups=groups, tiled=True)  5.23 us
    all_to_all x1, starting transfers between devices, per_device(): message = lax.all_to_all(message, 'tensor', 0, 0, tiled=True)  4.65 us
    all_to_all x1, waiting for transfers between devices, per_device(): lax.all_to_all(message, 'dp', 0, 0, axis_index_groups=groups, tiled=True)  3.92 us
    add x1, other arithmetic, per_device(): down_grad = total / jnp.float32(examples) + added_noise.astype(jnp.float32)  2.98 us
  transfers between devices with their start and end apart: 19, of which 11 were waited for; matrix products, arithmetic and copies ran while one was open for 9% of the time, Pallas kernels for 1%

profile of v3, /device:TPU:1, one launch (start us, length us, event | category | flops | bytes accessed | tf_op | source)
XLA Modules:
  0.0 122.3 jit_solution(9338139503770614520)
XLA Ops:
  0.6 1.5 %fusion.4.refs_5_ = bf16[128,1792]{1,0:T(8,128)(2,1)S(1)} fusion(bf16[128,1792]{1,0:T(8,128)(2,1)} %param.6, bf16[128,1792]{1,0:T(8,128)(2,1)} %param.5), kind=kLoop, calls=%fused_computation.12 | loop fusion | flops 1835008 | bytes 1376256 | tf_op jit(solution)/shard_map/convert_element_type | solution.py:197
  2.1 3.4 %collective-permute-start.1 = (bf16[128,1792]{1,0:T(8,128)(2,1)S(1)}, bf16[128,1792]{1,0:T(8,128)(2,1)S(1)}, u32[]{:S(2)}, u32[]{:S(2)}) collective-permute-start(bf16[128,1792]{1,0:T(8,128)(2,1)S(1)} %fusion.4.refs_5_), channel_id=1, source_target_pairs={{0,16},{1,17},{2,18},{3,19},{4,20},{5,21},{6,22},{7,23},{8,56},{9,... | collective-permute-start | bytes 1376264 | tf_op jit(solution)/shard_map/ppermute | solution.py:29
  5.5 6.0 %collective-permute-start = (bf16[128,1792]{1,0:T(8,128)(2,1)S(1)}, bf16[128,1792]{1,0:T(8,128)(2,1)S(1)}, u32[]{:S(2)}, u32[]{:S(2)}) collective-permute-start(bf16[128,1792]{1,0:T(8,128)(2,1)S(1)} %fusion.4.refs_5_), channel_id=1, source_target_pairs={{0,64},{1,65},{2,66},{3,67},{4,68},{5,69},{6,70},{7,71},{8,200},{9... | collective-permute-start | bytes 1376264 | tf_op jit(solution)/shard_map/ppermute | solution.py:29
  11.5 1.2 %convolution_bitcast_fusion.1 = f32[1,2,8,8,64]{4,3,2,1,0:T(8,128)S(1)} fusion(bf16[2,64,1024]{2,1,0:T(8,128)(2,1)} %bitcast.49), kind=kOutput, calls=%fused_computation.4 | convolution fusion | flops 16777216 | bytes 294912 | tf_op jit(solution)/shard_map/btf,buf->btu/dot_general | solution.py:204
  14.2 4.6 %all-to-all-start = ((bf16[8,24,1024]{2,1,0:T(8,128)(2,1)}), bf16[8,24,1024]{2,1,0:T(8,128)(2,1)S(1)}, u32[]{:S(2)}, u32[]{:S(2)}) async-start(bf16[8,24,1024]{2,1,0:T(8,128)(2,1)} %pad_maximum_fusion.4), calls=%async_computation | async-start | bytes 786432 | tf_op jit(solution)/shard_map/all_to_all | solution.py:219
  19.5 1.7 %collective-permute-done._.refs_9_ = bf16[128,1792]{1,0:T(8,128)(2,1)S(1)} collective-permute-done((bf16[128,1792]{1,0:T(8,128)(2,1)S(1)}, bf16[128,1792]{1,0:T(8,128)(2,1)S(1)}, u32[]{:S(2)}, u32[]{:S(2)}) %collective-permute-start) | collective-permute-done | bytes 458784 | tf_op jit(solution)/shard_map/ppermute | solution.py:29
  21.3 0.8 copy-done.13
  22.7 5.2 %all-to-all-done = bf16[8,24,1024]{2,1,0:T(8,128)(2,1)S(1)} async-done(((bf16[8,24,1024]{2,1,0:T(8,128)(2,1)}), bf16[8,24,1024]{2,1,0:T(8,128)(2,1)S(1)}, u32[]{:S(2)}, u32[]{:S(2)}) %all-to-all-start) | async-done | bytes 393248 | tf_op jit(solution)/shard_map/all_to_all | solution.py:219
  28.4 2.7 %collective-permute-start.3 = (bf16[128,1792]{1,0:T(8,128)(2,1)}, bf16[128,1792]{1,0:T(8,128)(2,1)S(1)}, u32[]{:S(2)}, u32[]{:S(2)}) collective-permute-start(bf16[128,1792]{1,0:T(8,128)(2,1)} %copy-done.13), channel_id=1, source_target_pairs={{0,64},{1,65},{2,66},{3,67},{4,68},{5,69},{6,70},{7,71},{8,200},{9... | collective-permute-start | bytes 1376264 | tf_op jit(solution)/shard_map/ppermute | solution.py:29
  31.1 4.4 %collective-permute-done.5.refs_8_ = bf16[128,1792]{1,0:T(8,128)(2,1)S(1)} collective-permute-done((bf16[128,1792]{1,0:T(8,128)(2,1)S(1)}, bf16[128,1792]{1,0:T(8,128)(2,1)S(1)}, u32[]{:S(2)}, u32[]{:S(2)}) %collective-permute-start.5) | collective-permute-done | bytes 458784 | tf_op jit(solution)/shard_map/ppermute | solution.py:29
  36.8 5.2 %all-to-all-start.1 = ((bf16[16,24,512]{2,1,0:T(8,128)(2,1)}), bf16[16,24,512]{2,1,0:T(8,128)(2,1)S(1)}, u32[]{:S(2)}, u32[]{:S(2)}) async-start(bf16[16,24,512]{2,1,0:T(8,128)(2,1)} %pad_maximum_fusion.5), calls=%async_computation.1 | async-start | bytes 786432 | tf_op jit(solution)/shard_map/all_to_all | solution.py:236
  42.1 1.1 pad_maximum_fusion
  43.2 2.6 %collective-permute-start.6 = (bf16[256,1792]{1,0:T(8,128)(2,1)}, bf16[256,1792]{1,0:T(8,128)(2,1)S(1)}, u32[]{:S(2)}, u32[]{:S(2)}) collective-permute-start(bf16[256,1792]{1,0:T(8,128)(2,1)} %pad_maximum_fusion), channel_id=1, source_target_pairs={{0,16},{1,17},{2,18},{3,19},{4,20},{5,21},{6,22},{7,23},{8,56},{9,... | collective-permute-start | bytes 2752520 | tf_op jit(solution)/shard_map/ppermute | solution.py:29
  45.8 3.3 %collective-permute-start.7 = (bf16[128,1792]{1,0:T(8,128)(2,1)S(1)}, bf16[128,1792]{1,0:T(8,128)(2,1)S(1)}, u32[]{:S(2)}, u32[]{:S(2)}) collective-permute-start(bf16[128,1792]{1,0:T(8,128)(2,1)S(1)} %collective-permute-done.3.refs_13_), channel_id=1, source_target_pairs={{0,64},{1,65},{2,66},{3,67},{4,68},{5,69},{6,70},{7,71},{8,200},{9... | collective-permute-start | bytes 1376264 | tf_op jit(solution)/shard_map/ppermute | solution.py:29
  49.1 3.9 %all-to-all-done.1 = bf16[16,24,512]{2,1,0:T(8,128)(2,1)S(1)} async-done(((bf16[16,24,512]{2,1,0:T(8,128)(2,1)}), bf16[16,24,512]{2,1,0:T(8,128)(2,1)S(1)}, u32[]{:S(2)}, u32[]{:S(2)}) %all-to-all-start.1) | async-done | bytes 393248 | tf_op jit(solution)/shard_map/all_to_all | solution.py:236
  53.2 5.3 %collective-permute-start.8 = (bf16[272,512]{1,0:T(8,128)(2,1)S(1)}, bf16[272,512]{1,0:T(8,128)(2,1)S(1)}, u32[]{:S(2)}, u32[]{:S(2)}) collective-permute-start(bf16[272,512]{1,0:T(8,128)(2,1)S(1)} %get-tuple-element.47), channel_id=1, source_target_pairs={{0,4},{1,5},{2,6},{3,7},{4,0},{5,1},{6,2},{7,3},{8,12},{9,13},{10,... | collective-permute-start | bytes 835592 | tf_op jit(solution)/shard_map/ppermute | solution.py:29
  58.5 1.1 collective-permute-done.6.refs_11_.refs_14_
  59.7 4.4 %collective-permute-done.7.refs_17_ = bf16[128,1792]{1,0:T(8,128)(2,1)S(1)} collective-permute-done((bf16[128,1792]{1,0:T(8,128)(2,1)S(1)}, bf16[128,1792]{1,0:T(8,128)(2,1)S(1)}, u32[]{:S(2)}, u32[]{:S(2)}) %collective-permute-start.7) | collective-permute-done | bytes 458784 | tf_op jit(solution)/shard_map/ppermute | solution.py:29
  64.2 3.9 %collective-permute-done.8 = bf16[272,512]{1,0:T(8,128)(2,1)S(1)} collective-permute-done((bf16[272,512]{1,0:T(8,128)(2,1)S(1)}, bf16[272,512]{1,0:T(8,128)(2,1)S(1)}, u32[]{:S(2)}, u32[]{:S(2)}) %collective-permute-start.8) | collective-permute-done | bytes 278560 | tf_op jit(solution)/shard_map/ppermute | solution.py:29
  68.2 2.6 %collective-permute-start.10 = (bf16[256,1792]{1,0:T(8,128)(2,1)S(1)}, bf16[256,1792]{1,0:T(8,128)(2,1)S(1)}, u32[]{:S(2)}, u32[]{:S(2)}) collective-permute-start(bf16[256,1792]{1,0:T(8,128)(2,1)S(1)} %pad_maximum_fusion.1), channel_id=1, source_target_pairs={{0,16},{1,17},{2,18},{3,19},{4,20},{5,21},{6,22},{7,23},{8,56},{9,... | collective-permute-start | bytes 2752520 | tf_op jit(solution)/shard_map/ppermute | solution.py:29
  71.2 1.0 collective-permute-start.11
  72.3 1.0 collective-permute-start.9
  73.3 8.1 %collective-permute-done.10.refs_15_.refs_18_ = bf16[256,1792]{1,0:T(8,128)(2,1)S(1)} collective-permute-done((bf16[256,1792]{1,0:T(8,128)(2,1)S(1)}, bf16[256,1792]{1,0:T(8,128)(2,1)S(1)}, u32[]{:S(2)}, u32[]{:S(2)}) %collective-permute-start.10) | collective-permute-done | bytes 917536 | tf_op jit(solution)/shard_map/ppermute | solution.py:29
  81.4 1.1 pad_maximum_fusion.2
  82.5 4.2 %collective-permute-done.9.refs_20_ = bf16[128,1792]{1,0:T(8,128)(2,1)S(1)} collective-permute-done((bf16[128,1792]{1,0:T(8,128)(2,1)S(1)}, bf16[128,1792]{1,0:T(8,128)(2,1)S(1)}, u32[]{:S(2)}, u32[]{:S(2)}) %collective-permute-start.9) | collective-permute-done | bytes 458784 | tf_op jit(solution)/shard_map/ppermute | solution.py:29
  86.7 0.9 collective-permute-start.14
  87.6 0.8 collective-permute-start.15
  89.7 12.2 %collective-permute-done.15._.refs_16_ = bf16[128,1792]{1,0:T(8,128)(2,1)S(1)} collective-permute-done((bf16[128,1792]{1,0:T(8,128)(2,1)S(1)}, bf16[128,1792]{1,0:T(8,128)(2,1)S(1)}, u32[]{:S(2)}, u32[]{:S(2)}) %collective-permute-start.15) | collective-permute-done | bytes 458784 | tf_op jit(solution)/shard_map/ppermute | solution.py:29
  103.2 0.9 copy-done.3
  104.1 9.7 %shard_map.70 = (f32[256,1792]{1,0:T(8,128)}, f32[256,1792]{1,0:T(8,128)}) custom-call(s32[19]{0:T(128)} %stack.97.refs_0_, bf16[2,272,512]{2,1,0:T(8,128)(2,1)} %copy-done.4, bf16[2,272,512]{2,1,0:T(8,128)(2,1)} %copy-done.11, bf16[2,272,512]{2,1,0:T(8,128)(2,1)} %collective-permute-done.13.refs_3_, bf16[2,272,512]{2,1,0:T(8,128)(2,1)} %copy-done.10, ...), custom_call_target="tpu_custom_call" | custom-call | flops 1048576 | bytes 1048576 | tf_op jit(solution)/shard_map/pallas_call | solution.py:138
  113.8 1.9 %collective-permute-start.16 = (f32[256,1792]{1,0:T(8,128)}, f32[256,1792]{1,0:T(8,128)S(1)}, u32[]{:S(2)}, u32[]{:S(2)}) collective-permute-start(f32[256,1792]{1,0:T(8,128)} %get-tuple-element.41), channel_id=1, source_target_pairs={{0,8},{1,9},{2,10},{3,11},{4,12},{5,13},{6,14},{7,15},{8,0},{9,1},... | collective-permute-start | bytes 5505032 | tf_op jit(solution)/shard_map/ppermute | solution.py:29
  119.3 3.0 %convert_add_fusion = f32[256,1792]{1,0:T(8,128)} fusion(bf16[256,1792]{1,0:T(8,128)(2,1)S(1)} %copy-done.9, f32[256,1792]{1,0:T(8,128)} %get-tuple-element.40, f32[256,1792]{1,0:T(8,128)S(1)} %collective-permute-done.16), kind=kLoop, calls=%fused_computation | loop fusion | flops 1835008 | bytes 6422528 | tf_op jit(solution)/shard_map/add | solution.py:271
  (100 shorter events, 11.5 us)
Async XLA Ops:
  0.6 12.8 %copy-start.5 = (bf16[128,1024]{1,0:T(8,128)(2,1)S(1)}, bf16[128,1024]{1,0:T(8,128)(2,1)}, u32[]{:S(2)}) copy-start(bf16[128,1024]{1,0:T(8,128)(2,1)} %param.7) | copy-start | bytes 786436
  2.1 12.1 %copy-start.1 = (bf16[128,1792]{1,0:T(8,128)(2,1)}, bf16[128,1792]{1,0:T(8,128)(2,1)S(1)}, u32[]{:S(2)}) copy-start(bf16[128,1792]{1,0:T(8,128)(2,1)S(1)} %fusion.4.refs_5_) | copy-start | bytes 1376260
  2.1 16.8 %collective-permute-start.1 = (bf16[128,1792]{1,0:T(8,128)(2,1)S(1)}, bf16[128,1792]{1,0:T(8,128)(2,1)S(1)}, u32[]{:S(2)}, u32[]{:S(2)}) collective-permute-start(bf16[128,1792]{1,0:T(8,128)(2,1)S(1)} %fusion.4.refs_5_), channel_id=1, source_target_pairs={{0,16},{1,17},{2,18},{3,19},{4,20},{5,21},{6,22},{7,23},{8,56},{9,... | collective-permute-start | bytes 1376264 | tf_op jit(solution)/shard_map/ppermute | solution.py:29
  5.5 15.8 %collective-permute-start = (bf16[128,1792]{1,0:T(8,128)(2,1)S(1)}, bf16[128,1792]{1,0:T(8,128)(2,1)S(1)}, u32[]{:S(2)}, u32[]{:S(2)}) collective-permute-start(bf16[128,1792]{1,0:T(8,128)(2,1)S(1)} %fusion.4.refs_5_), channel_id=1, source_target_pairs={{0,64},{1,65},{2,66},{3,67},{4,68},{5,69},{6,70},{7,71},{8,200},{9... | collective-permute-start | bytes 1376264 | tf_op jit(solution)/shard_map/ppermute | solution.py:29
  14.2 13.7 %all-to-all-start = ((bf16[8,24,1024]{2,1,0:T(8,128)(2,1)}), bf16[8,24,1024]{2,1,0:T(8,128)(2,1)S(1)}, u32[]{:S(2)}, u32[]{:S(2)}) async-start(bf16[8,24,1024]{2,1,0:T(8,128)(2,1)} %pad_maximum_fusion.4), calls=%async_computation | async-start | bytes 786432 | tf_op jit(solution)/shard_map/all_to_all | solution.py:219
  18.9 16.9 %copy-start.19 = (f32[2]{0:T(128)S(1)}, f32[2]{0:T(128)}, u32[]{:S(2)}) copy-start(f32[2]{0:T(128)} %param.8) | copy-start | bytes 28
  18.9 9.0 %collective-permute-start.2 = (bf16[128,1792]{1,0:T(8,128)(2,1)S(1)}, bf16[128,1792]{1,0:T(8,128)(2,1)S(1)}, u32[]{:S(2)}, u32[]{:S(2)}) collective-permute-start(bf16[128,1792]{1,0:T(8,128)(2,1)S(1)} %collective-permute-done.1.refs_6_), channel_id=1, source_target_pairs={{0,16},{1,17},{2,18},{3,19},{4,20},{5,21},{6,22},{7,23},{8,56},{9,... | collective-permute-start | bytes 1376264 | tf_op jit(solution)/shard_map/ppermute | solution.py:29
  27.9 7.6 %copy-start.14 = (bf16[128,1792]{1,0:T(8,128)(2,1)}, bf16[128,1792]{1,0:T(8,128)(2,1)S(1)}, u32[]{:S(2)}) copy-start(bf16[128,1792]{1,0:T(8,128)(2,1)S(1)} %collective-permute-done.2.refs_7_) | copy-start | bytes 1376260
  27.9 7.6 %collective-permute-start.5 = (bf16[128,1792]{1,0:T(8,128)(2,1)S(1)}, bf16[128,1792]{1,0:T(8,128)(2,1)S(1)}, u32[]{:S(2)}, u32[]{:S(2)}) collective-permute-start(bf16[128,1792]{1,0:T(8,128)(2,1)S(1)} %collective-permute-done.2.refs_7_), channel_id=1, source_target_pairs={{0,16},{1,17},{2,18},{3,19},{4,20},{5,21},{6,22},{7,23},{8,56},{9,... | collective-permute-start | bytes 1376264 | tf_op jit(solution)/shard_map/ppermute | solution.py:29
  28.4 13.6 %collective-permute-start.3 = (bf16[128,1792]{1,0:T(8,128)(2,1)}, bf16[128,1792]{1,0:T(8,128)(2,1)S(1)}, u32[]{:S(2)}, u32[]{:S(2)}) collective-permute-start(bf16[128,1792]{1,0:T(8,128)(2,1)} %copy-done.13), channel_id=1, source_target_pairs={{0,64},{1,65},{2,66},{3,67},{4,68},{5,69},{6,70},{7,71},{8,200},{9... | collective-permute-start | bytes 1376264 | tf_op jit(solution)/shard_map/ppermute | solution.py:29
  31.1 11.0 %collective-permute-start.4 = (bf16[128,1792]{1,0:T(8,128)(2,1)}, bf16[128,1792]{1,0:T(8,128)(2,1)S(1)}, u32[]{:S(2)}, u32[]{:S(2)}) collective-permute-start(bf16[128,1792]{1,0:T(8,128)(2,1)} %copy-done.13), channel_id=1, source_target_pairs={{0,16},{1,17},{2,18},{3,19},{4,20},{5,21},{6,22},{7,23},{8,56},{9,... | collective-permute-start | bytes 1376264 | tf_op jit(solution)/shard_map/ppermute | solution.py:29
  36.8 16.2 %all-to-all-start.1 = ((bf16[16,24,512]{2,1,0:T(8,128)(2,1)}), bf16[16,24,512]{2,1,0:T(8,128)(2,1)S(1)}, u32[]{:S(2)}, u32[]{:S(2)}) async-start(bf16[16,24,512]{2,1,0:T(8,128)(2,1)} %pad_maximum_fusion.5), calls=%async_computation.1 | async-start | bytes 786432 | tf_op jit(solution)/shard_map/all_to_all | solution.py:236
  42.1 17.6 %copy-start.6 = (bf16[128,1792]{1,0:T(8,128)(2,1)}, bf16[128,1792]{1,0:T(8,128)(2,1)S(1)}, u32[]{:S(2)}) copy-start(bf16[128,1792]{1,0:T(8,128)(2,1)S(1)} %collective-permute-done.3.refs_13_) | copy-start | bytes 1376260
  42.1 17.6 %copy-start.7 = (bf16[128,1792]{1,0:T(8,128)(2,1)}, bf16[128,1792]{1,0:T(8,128)(2,1)S(1)}, u32[]{:S(2)}) copy-start(bf16[128,1792]{1,0:T(8,128)(2,1)S(1)} %collective-permute-done.4.refs_10_) | copy-start | bytes 1376260
  43.2 16.4 %collective-permute-start.6 = (bf16[256,1792]{1,0:T(8,128)(2,1)}, bf16[256,1792]{1,0:T(8,128)(2,1)S(1)}, u32[]{:S(2)}, u32[]{:S(2)}) collective-permute-start(bf16[256,1792]{1,0:T(8,128)(2,1)} %pad_maximum_fusion), channel_id=1, source_target_pairs={{0,16},{1,17},{2,18},{3,19},{4,20},{5,21},{6,22},{7,23},{8,56},{9,... | collective-permute-start | bytes 2752520 | tf_op jit(solution)/shard_map/ppermute | solution.py:29
  45.8 18.4 %collective-permute-start.7 = (bf16[128,1792]{1,0:T(8,128)(2,1)S(1)}, bf16[128,1792]{1,0:T(8,128)(2,1)S(1)}, u32[]{:S(2)}, u32[]{:S(2)}) collective-permute-start(bf16[128,1792]{1,0:T(8,128)(2,1)S(1)} %collective-permute-done.3.refs_13_), channel_id=1, source_target_pairs={{0,64},{1,65},{2,66},{3,67},{4,68},{5,69},{6,70},{7,71},{8,200},{9... | collective-permute-start | bytes 1376264 | tf_op jit(solution)/shard_map/ppermute | solution.py:29
  53.2 14.9 %collective-permute-start.8 = (bf16[272,512]{1,0:T(8,128)(2,1)S(1)}, bf16[272,512]{1,0:T(8,128)(2,1)S(1)}, u32[]{:S(2)}, u32[]{:S(2)}) collective-permute-start(bf16[272,512]{1,0:T(8,128)(2,1)S(1)} %get-tuple-element.47), channel_id=1, source_target_pairs={{0,4},{1,5},{2,6},{3,7},{4,0},{5,1},{6,2},{7,3},{8,12},{9,13},{10,... | collective-permute-start | bytes 835592 | tf_op jit(solution)/shard_map/ppermute | solution.py:29
  59.6 4.6 %copy-start = (bf16[256,1792]{1,0:T(8,128)(2,1)}, bf16[256,1792]{1,0:T(8,128)(2,1)S(1)}, u32[]{:S(2)}) copy-start(bf16[256,1792]{1,0:T(8,128)(2,1)S(1)} %collective-permute-done.6.refs_11_.refs_14_) | copy-start | bytes 2752516
  59.7 12.6 %copy-start.16 = (bf16[128,1792]{1,0:T(8,128)(2,1)S(1)}, bf16[128,1792]{1,0:T(8,128)(2,1)}, u32[]{:S(2)}) copy-start(bf16[128,1792]{1,0:T(8,128)(2,1)} %copy-done.15) | copy-start | bytes 1376260
  64.1 9.1 %copy-start.8 = (bf16[128,1792]{1,0:T(8,128)(2,1)}, bf16[128,1792]{1,0:T(8,128)(2,1)S(1)}, u32[]{:S(2)}) copy-start(bf16[128,1792]{1,0:T(8,128)(2,1)S(1)} %collective-permute-done.7.refs_17_) | copy-start | bytes 1376260
  68.2 35.0 %copy-start.4 = (bf16[2,272,512]{2,1,0:T(8,128)(2,1)}, bf16[2,272,512]{2,1,0:T(8,128)(2,1)S(1)}, u32[]{:S(2)}) copy-start(bf16[2,272,512]{2,1,0:T(8,128)(2,1)S(1)} %pad_maximum_fusion.3.refs_1_) | copy-start | bytes 1671172
  68.2 13.2 %collective-permute-start.10 = (bf16[256,1792]{1,0:T(8,128)(2,1)S(1)}, bf16[256,1792]{1,0:T(8,128)(2,1)S(1)}, u32[]{:S(2)}, u32[]{:S(2)}) collective-permute-start(bf16[256,1792]{1,0:T(8,128)(2,1)S(1)} %pad_maximum_fusion.1), channel_id=1, source_target_pairs={{0,16},{1,17},{2,18},{3,19},{4,20},{5,21},{6,22},{7,23},{8,56},{9,... | collective-permute-start | bytes 2752520 | tf_op jit(solution)/shard_map/ppermute | solution.py:29
  70.8 15.9 %collective-permute-start.12 = (bf16[2,272,512]{2,1,0:T(8,128)(2,1)S(1)}, bf16[2,272,512]{2,1,0:T(8,128)(2,1)S(1)}, u32[]{:S(2)}, u32[]{:S(2)}) collective-permute-start(bf16[2,272,512]{2,1,0:T(8,128)(2,1)S(1)} %pad_maximum_fusion.3.refs_1_), channel_id=1, source_target_pairs={{0,3},{1,0},{2,1},{3,2},{4,7},{5,4},{6,5},{7,6},{8,11},{9,8},{10,9... | collective-permute-start | bytes 1671176 | tf_op jit(solution)/shard_map/ppermute | solution.py:29
  71.2 15.4 %collective-permute-start.11 = (bf16[2,272,512]{2,1,0:T(8,128)(2,1)S(1)}, bf16[2,272,512]{2,1,0:T(8,128)(2,1)S(1)}, u32[]{:S(2)}, u32[]{:S(2)}) collective-permute-start(bf16[2,272,512]{2,1,0:T(8,128)(2,1)S(1)} %pad_maximum_fusion.3.refs_1_), channel_id=1, source_target_pairs={{0,1},{1,2},{2,3},{3,0},{4,5},{5,6},{6,7},{7,4},{8,9},{9,10},{10,1... | collective-permute-start | bytes 1671176 | tf_op jit(solution)/shard_map/ppermute | solution.py:29
  72.3 14.4 %collective-permute-start.9 = (bf16[128,1792]{1,0:T(8,128)(2,1)S(1)}, bf16[128,1792]{1,0:T(8,128)(2,1)S(1)}, u32[]{:S(2)}, u32[]{:S(2)}) collective-permute-start(bf16[128,1792]{1,0:T(8,128)(2,1)S(1)} %copy-done.16), channel_id=1, source_target_pairs={{0,192},{1,193},{2,194},{3,195},{4,196},{5,197},{6,198},{7,199},{8... | collective-permute-start | bytes 1376264 | tf_op jit(solution)/shard_map/ppermute | solution.py:29
  81.4 21.8 %copy-start.2 = (bf16[256,1792]{1,0:T(8,128)(2,1)}, bf16[256,1792]{1,0:T(8,128)(2,1)S(1)}, u32[]{:S(2)}) copy-start(bf16[256,1792]{1,0:T(8,128)(2,1)S(1)} %collective-permute-done.10.refs_15_.refs_18_) | copy-start | bytes 2752516
  86.7 15.2 %copy-start.17 = (bf16[128,1792]{1,0:T(8,128)(2,1)}, bf16[128,1792]{1,0:T(8,128)(2,1)S(1)}, u32[]{:S(2)}) copy-start(bf16[128,1792]{1,0:T(8,128)(2,1)S(1)} %collective-permute-done.9.refs_20_) | copy-start | bytes 1376260
  86.7 16.5 %collective-permute-start.14 = (bf16[256,1792]{1,0:T(8,128)(2,1)}, bf16[256,1792]{1,0:T(8,128)(2,1)S(1)}, u32[]{:S(2)}, u32[]{:S(2)}) collective-permute-start(bf16[256,1792]{1,0:T(8,128)(2,1)} %pad_maximum_fusion.2), channel_id=1, source_target_pairs={{0,16},{1,17},{2,18},{3,19},{4,20},{5,21},{6,22},{7,23},{8,56},{9,... | collective-permute-start | bytes 2752520 | tf_op jit(solution)/shard_map/ppermute | solution.py:29
  87.6 14.3 %collective-permute-start.15 = (bf16[128,1792]{1,0:T(8,128)(2,1)S(1)}, bf16[128,1792]{1,0:T(8,128)(2,1)S(1)}, u32[]{:S(2)}, u32[]{:S(2)}) collective-permute-start(bf16[128,1792]{1,0:T(8,128)(2,1)S(1)} %collective-permute-done.9.refs_20_), channel_id=1, source_target_pairs={{0,192},{1,193},{2,194},{3,195},{4,196},{5,197},{6,198},{7,199},{8... | collective-permute-start | bytes 1376264 | tf_op jit(solution)/shard_map/ppermute | solution.py:29
  88.4 14.8 %collective-permute-start.13 = (bf16[2,272,512]{2,1,0:T(8,128)(2,1)S(1)}, bf16[2,272,512]{2,1,0:T(8,128)(2,1)}, u32[]{:S(2)}, u32[]{:S(2)}) collective-permute-start(bf16[2,272,512]{2,1,0:T(8,128)(2,1)S(1)} %pad_maximum_fusion.3.refs_1_), channel_id=1, source_target_pairs={{0,2},{1,3},{2,0},{3,1},{4,6},{5,7},{6,4},{7,5},{8,10},{9,11},{10,... | collective-permute-start | bytes 1671176 | tf_op jit(solution)/shard_map/ppermute | solution.py:29
  103.2 16.2 %copy-start.9 = (bf16[256,1792]{1,0:T(8,128)(2,1)S(1)}, bf16[256,1792]{1,0:T(8,128)(2,1)}, u32[]{:S(2)}) copy-start(bf16[256,1792]{1,0:T(8,128)(2,1)} %param.9) | copy-start | bytes 2752516
  113.8 5.5 %collective-permute-start.16 = (f32[256,1792]{1,0:T(8,128)}, f32[256,1792]{1,0:T(8,128)S(1)}, u32[]{:S(2)}, u32[]{:S(2)}) collective-permute-start(f32[256,1792]{1,0:T(8,128)} %get-tuple-element.41), channel_id=1, source_target_pairs={{0,8},{1,9},{2,10},{3,11},{4,12},{5,13},{6,14},{7,15},{8,0},{9,1},... | collective-permute-start | bytes 5505032 | tf_op jit(solution)/shard_map/ppermute | solution.py:29
  (7 other events, 10.1 us)

commit v4 on v3

--- a/solution.py
+++ b/solution.py
@@ -7,8 +7,8 @@
 
 D = 8192
 FF = 14336
-TILE = 896
-GROUP = 512
+TILE = 256
+GROUP = 1024
 
 DEVICES = [
     (zh, x, c, zl, y)

time: 123 us -> 123 us (level)
  no operation moved by 1% of the time
where the time goes in v4:
time: 123 us; the launch traced here: 122 us
  waiting for transfers between devices  49.4 us (40%)
  starting transfers between devices  43.4 us (35%)
  other arithmetic  11.2 us (9%)
  Pallas kernels  10.8 us (9%)
  local copies, waits for them, and re-layouts  4.87 us (4%)
  matrix products  1.48 us (1%)
    ppermute x17, waiting for transfers between devices, permute(): return lax.ppermute(value, ('dp', 'tensor'), pairs)  40.3 us
    ppermute x17, starting transfers between devices, permute(): return lax.ppermute(value, ('dp', 'tensor'), pairs)  33.6 us
    pallas_call x1, Pallas kernels, product(): pl.pallas_call(lambda *refs: product_kernel(layout, len(tokens), *refs),...  9.59 us
    all_to_all x1, waiting for transfers between devices, per_device(): message = lax.all_to_all(message, 'tensor', 0, 0, tiled=True)  5.24 us
    all_to_all x1, starting transfers between devices, per_device(): lax.all_to_all(message, 'dp', 0, 0, axis_index_groups=groups, tiled=True)  5.23 us
    all_to_all x1, starting transfers between devices, per_device(): message = lax.all_to_all(message, 'tensor', 0, 0, tiled=True)  4.65 us
    all_to_all x1, waiting for transfers between devices, per_device(): lax.all_to_all(message, 'dp', 0, 0, axis_index_groups=groups, tiled=True)  3.94 us
    add x1, other arithmetic, per_device(): down_grad = total / jnp.float32(examples) + added_noise.astype(jnp.float32)  2.98 us
  transfers between devices with their start and end apart: 19, of which 11 were waited for; matrix products, arithmetic and copies ran while one was open for 9% of the time, Pallas kernels for 1%

profile of v4, /device:TPU:1, one launch (start us, length us, event | category | flops | bytes accessed | tf_op | source)
XLA Modules:
  0.0 122.2 jit_solution(16426271686412169957)
XLA Ops:
  0.6 1.5 %fusion.4.refs_5_ = bf16[128,1792]{1,0:T(8,128)(2,1)S(1)} fusion(bf16[128,1792]{1,0:T(8,128)(2,1)} %param.6, bf16[128,1792]{1,0:T(8,128)(2,1)} %param.5), kind=kLoop, calls=%fused_computation.12 | loop fusion | flops 1835008 | bytes 1376256 | tf_op jit(solution)/shard_map/convert_element_type | solution.py:197
  2.1 3.4 %collective-permute-start.1 = (bf16[128,1792]{1,0:T(8,128)(2,1)S(1)}, bf16[128,1792]{1,0:T(8,128)(2,1)S(1)}, u32[]{:S(2)}, u32[]{:S(2)}) collective-permute-start(bf16[128,1792]{1,0:T(8,128)(2,1)S(1)} %fusion.4.refs_5_), channel_id=1, source_target_pairs={{0,16},{1,17},{2,18},{3,19},{4,20},{5,21},{6,22},{7,23},{8,56},{9,... | collective-permute-start | bytes 1376264 | tf_op jit(solution)/shard_map/ppermute | solution.py:29
  5.5 6.0 %collective-permute-start = (bf16[128,1792]{1,0:T(8,128)(2,1)S(1)}, bf16[128,1792]{1,0:T(8,128)(2,1)S(1)}, u32[]{:S(2)}, u32[]{:S(2)}) collective-permute-start(bf16[128,1792]{1,0:T(8,128)(2,1)S(1)} %fusion.4.refs_5_), channel_id=1, source_target_pairs={{0,64},{1,65},{2,66},{3,67},{4,68},{5,69},{6,70},{7,71},{8,200},{9... | collective-permute-start | bytes 1376264 | tf_op jit(solution)/shard_map/ppermute | solution.py:29
  11.5 1.2 %convolution_bitcast_fusion.1 = f32[1,2,8,8,64]{4,3,2,1,0:T(8,128)S(1)} fusion(bf16[2,64,1024]{2,1,0:T(8,128)(2,1)} %bitcast.49), kind=kOutput, calls=%fused_computation.4 | convolution fusion | flops 16777216 | bytes 294912 | tf_op jit(solution)/shard_map/btf,buf->btu/dot_general | solution.py:204
  14.2 4.6 %all-to-all-start = ((bf16[8,24,1024]{2,1,0:T(8,128)(2,1)}), bf16[8,24,1024]{2,1,0:T(8,128)(2,1)S(1)}, u32[]{:S(2)}, u32[]{:S(2)}) async-start(bf16[8,24,1024]{2,1,0:T(8,128)(2,1)} %pad_maximum_fusion.4), calls=%async_computation | async-start | bytes 786432 | tf_op jit(solution)/shard_map/all_to_all | solution.py:219
  19.5 1.7 %collective-permute-done._.refs_9_ = bf16[128,1792]{1,0:T(8,128)(2,1)S(1)} collective-permute-done((bf16[128,1792]{1,0:T(8,128)(2,1)S(1)}, bf16[128,1792]{1,0:T(8,128)(2,1)S(1)}, u32[]{:S(2)}, u32[]{:S(2)}) %collective-permute-start) | collective-permute-done | bytes 458784 | tf_op jit(solution)/shard_map/ppermute | solution.py:29
  21.3 0.8 copy-done.13
  22.7 5.2 %all-to-all-done = bf16[8,24,1024]{2,1,0:T(8,128)(2,1)S(1)} async-done(((bf16[8,24,1024]{2,1,0:T(8,128)(2,1)}), bf16[8,24,1024]{2,1,0:T(8,128)(2,1)S(1)}, u32[]{:S(2)}, u32[]{:S(2)}) %all-to-all-start) | async-done | bytes 393248 | tf_op jit(solution)/shard_map/all_to_all | solution.py:219
  28.4 2.7 %collective-permute-start.3 = (bf16[128,1792]{1,0:T(8,128)(2,1)}, bf16[128,1792]{1,0:T(8,128)(2,1)S(1)}, u32[]{:S(2)}, u32[]{:S(2)}) collective-permute-start(bf16[128,1792]{1,0:T(8,128)(2,1)} %copy-done.13), channel_id=1, source_target_pairs={{0,64},{1,65},{2,66},{3,67},{4,68},{5,69},{6,70},{7,71},{8,200},{9... | collective-permute-start | bytes 1376264 | tf_op jit(solution)/shard_map/ppermute | solution.py:29
  31.1 4.4 %collective-permute-done.5.refs_8_ = bf16[128,1792]{1,0:T(8,128)(2,1)S(1)} collective-permute-done((bf16[128,1792]{1,0:T(8,128)(2,1)S(1)}, bf16[128,1792]{1,0:T(8,128)(2,1)S(1)}, u32[]{:S(2)}, u32[]{:S(2)}) %collective-permute-start.5) | collective-permute-done | bytes 458784 | tf_op jit(solution)/shard_map/ppermute | solution.py:29
  36.8 5.2 %all-to-all-start.1 = ((bf16[16,24,512]{2,1,0:T(8,128)(2,1)}), bf16[16,24,512]{2,1,0:T(8,128)(2,1)S(1)}, u32[]{:S(2)}, u32[]{:S(2)}) async-start(bf16[16,24,512]{2,1,0:T(8,128)(2,1)} %pad_maximum_fusion.5), calls=%async_computation.1 | async-start | bytes 786432 | tf_op jit(solution)/shard_map/all_to_all | solution.py:236
  42.1 1.1 pad_maximum_fusion
  43.2 2.6 %collective-permute-start.6 = (bf16[256,1792]{1,0:T(8,128)(2,1)}, bf16[256,1792]{1,0:T(8,128)(2,1)S(1)}, u32[]{:S(2)}, u32[]{:S(2)}) collective-permute-start(bf16[256,1792]{1,0:T(8,128)(2,1)} %pad_maximum_fusion), channel_id=1, source_target_pairs={{0,16},{1,17},{2,18},{3,19},{4,20},{5,21},{6,22},{7,23},{8,56},{9,... | collective-permute-start | bytes 2752520 | tf_op jit(solution)/shard_map/ppermute | solution.py:29
  45.7 3.3 %collective-permute-start.7 = (bf16[128,1792]{1,0:T(8,128)(2,1)S(1)}, bf16[128,1792]{1,0:T(8,128)(2,1)S(1)}, u32[]{:S(2)}, u32[]{:S(2)}) collective-permute-start(bf16[128,1792]{1,0:T(8,128)(2,1)S(1)} %collective-permute-done.3.refs_13_), channel_id=1, source_target_pairs={{0,64},{1,65},{2,66},{3,67},{4,68},{5,69},{6,70},{7,71},{8,200},{9... | collective-permute-start | bytes 1376264 | tf_op jit(solution)/shard_map/ppermute | solution.py:29
  49.0 3.9 %all-to-all-done.1 = bf16[16,24,512]{2,1,0:T(8,128)(2,1)S(1)} async-done(((bf16[16,24,512]{2,1,0:T(8,128)(2,1)}), bf16[16,24,512]{2,1,0:T(8,128)(2,1)S(1)}, u32[]{:S(2)}, u32[]{:S(2)}) %all-to-all-start.1) | async-done | bytes 393248 | tf_op jit(solution)/shard_map/all_to_all | solution.py:236
  53.2 5.3 %collective-permute-start.8 = (bf16[272,512]{1,0:T(8,128)(2,1)S(1)}, bf16[272,512]{1,0:T(8,128)(2,1)S(1)}, u32[]{:S(2)}, u32[]{:S(2)}) collective-permute-start(bf16[272,512]{1,0:T(8,128)(2,1)S(1)} %get-tuple-element.47), channel_id=1, source_target_pairs={{0,4},{1,5},{2,6},{3,7},{4,0},{5,1},{6,2},{7,3},{8,12},{9,13},{10,... | collective-permute-start | bytes 835592 | tf_op jit(solution)/shard_map/ppermute | solution.py:29
  58.5 1.1 collective-permute-done.6.refs_11_.refs_14_
  59.7 4.4 %collective-permute-done.7.refs_17_ = bf16[128,1792]{1,0:T(8,128)(2,1)S(1)} collective-permute-done((bf16[128,1792]{1,0:T(8,128)(2,1)S(1)}, bf16[128,1792]{1,0:T(8,128)(2,1)S(1)}, u32[]{:S(2)}, u32[]{:S(2)}) %collective-permute-start.7) | collective-permute-done | bytes 458784 | tf_op jit(solution)/shard_map/ppermute | solution.py:29
  64.2 3.9 %collective-permute-done.8 = bf16[272,512]{1,0:T(8,128)(2,1)S(1)} collective-permute-done((bf16[272,512]{1,0:T(8,128)(2,1)S(1)}, bf16[272,512]{1,0:T(8,128)(2,1)S(1)}, u32[]{:S(2)}, u32[]{:S(2)}) %collective-permute-start.8) | collective-permute-done | bytes 278560 | tf_op jit(solution)/shard_map/ppermute | solution.py:29
  68.1 2.7 %collective-permute-start.10 = (bf16[256,1792]{1,0:T(8,128)(2,1)S(1)}, bf16[256,1792]{1,0:T(8,128)(2,1)S(1)}, u32[]{:S(2)}, u32[]{:S(2)}) collective-permute-start(bf16[256,1792]{1,0:T(8,128)(2,1)S(1)} %pad_maximum_fusion.1), channel_id=1, source_target_pairs={{0,16},{1,17},{2,18},{3,19},{4,20},{5,21},{6,22},{7,23},{8,56},{9,... | collective-permute-start | bytes 2752520 | tf_op jit(solution)/shard_map/ppermute | solution.py:29
  71.2 1.0 collective-permute-start.11
  72.3 1.0 collective-permute-start.9
  73.3 8.0 %collective-permute-done.10.refs_15_.refs_18_ = bf16[256,1792]{1,0:T(8,128)(2,1)S(1)} collective-permute-done((bf16[256,1792]{1,0:T(8,128)(2,1)S(1)}, bf16[256,1792]{1,0:T(8,128)(2,1)S(1)}, u32[]{:S(2)}, u32[]{:S(2)}) %collective-permute-start.10) | collective-permute-done | bytes 917536 | tf_op jit(solution)/shard_map/ppermute | solution.py:29
  81.3 1.1 pad_maximum_fusion.2
  82.4 4.3 %collective-permute-done.9.refs_20_ = bf16[128,1792]{1,0:T(8,128)(2,1)S(1)} collective-permute-done((bf16[128,1792]{1,0:T(8,128)(2,1)S(1)}, bf16[128,1792]{1,0:T(8,128)(2,1)S(1)}, u32[]{:S(2)}, u32[]{:S(2)}) %collective-permute-start.9) | collective-permute-done | bytes 458784 | tf_op jit(solution)/shard_map/ppermute | solution.py:29
  86.7 0.9 collective-permute-start.14
  89.7 12.2 %collective-permute-done.15._.refs_16_ = bf16[128,1792]{1,0:T(8,128)(2,1)S(1)} collective-permute-done((bf16[128,1792]{1,0:T(8,128)(2,1)S(1)}, bf16[128,1792]{1,0:T(8,128)(2,1)S(1)}, u32[]{:S(2)}, u32[]{:S(2)}) %collective-permute-start.15) | collective-permute-done | bytes 458784 | tf_op jit(solution)/shard_map/ppermute | solution.py:29
  103.2 0.9 copy-done.3
  104.1 9.6 %shard_map.70 = (f32[256,1792]{1,0:T(8,128)}, f32[256,1792]{1,0:T(8,128)}) custom-call(s32[19]{0:T(128)} %stack.97.refs_0_, bf16[2,272,512]{2,1,0:T(8,128)(2,1)} %copy-done.4, bf16[2,272,512]{2,1,0:T(8,128)(2,1)} %copy-done.11, bf16[2,272,512]{2,1,0:T(8,128)(2,1)} %collective-permute-done.13.refs_3_, bf16[2,272,512]{2,1,0:T(8,128)(2,1)} %copy-done.10, ...), custom_call_target="tpu_custom_call" | custom-call | flops 1048576 | bytes 1048576 | tf_op jit(solution)/shard_map/pallas_call | solution.py:138
  113.7 1.8 %collective-permute-start.16 = (f32[256,1792]{1,0:T(8,128)}, f32[256,1792]{1,0:T(8,128)S(1)}, u32[]{:S(2)}, u32[]{:S(2)}) collective-permute-start(f32[256,1792]{1,0:T(8,128)} %get-tuple-element.41), channel_id=1, source_target_pairs={{0,8},{1,9},{2,10},{3,11},{4,12},{5,13},{6,14},{7,15},{8,0},{9,1},... | collective-permute-start | bytes 5505032 | tf_op jit(solution)/shard_map/ppermute | solution.py:29
  116.3 0.8 convert_reduce_fusion.1
  119.2 3.0 %convert_add_fusion = f32[256,1792]{1,0:T(8,128)} fusion(bf16[256,1792]{1,0:T(8,128)(2,1)S(1)} %copy-done.9, f32[256,1792]{1,0:T(8,128)} %get-tuple-element.40, f32[256,1792]{1,0:T(8,128)S(1)} %collective-permute-done.16), kind=kLoop, calls=%fused_computation | loop fusion | flops 1835008 | bytes 6422528 | tf_op jit(solution)/shard_map/add | solution.py:271
  (100 shorter events, 11.6 us)
Async XLA Ops:
  0.6 12.8 %copy-start.5 = (bf16[128,1024]{1,0:T(8,128)(2,1)S(1)}, bf16[128,1024]{1,0:T(8,128)(2,1)}, u32[]{:S(2)}) copy-start(bf16[128,1024]{1,0:T(8,128)(2,1)} %param.7) | copy-start | bytes 786436
  2.1 12.1 %copy-start.1 = (bf16[128,1792]{1,0:T(8,128)(2,1)}, bf16[128,1792]{1,0:T(8,128)(2,1)S(1)}, u32[]{:S(2)}) copy-start(bf16[128,1792]{1,0:T(8,128)(2,1)S(1)} %fusion.4.refs_5_) | copy-start | bytes 1376260
  2.1 16.8 %collective-permute-start.1 = (bf16[128,1792]{1,0:T(8,128)(2,1)S(1)}, bf16[128,1792]{1,0:T(8,128)(2,1)S(1)}, u32[]{:S(2)}, u32[]{:S(2)}) collective-permute-start(bf16[128,1792]{1,0:T(8,128)(2,1)S(1)} %fusion.4.refs_5_), channel_id=1, source_target_pairs={{0,16},{1,17},{2,18},{3,19},{4,20},{5,21},{6,22},{7,23},{8,56},{9,... | collective-permute-start | bytes 1376264 | tf_op jit(solution)/shard_map/ppermute | solution.py:29
  5.5 15.8 %collective-permute-start = (bf16[128,1792]{1,0:T(8,128)(2,1)S(1)}, bf16[128,1792]{1,0:T(8,128)(2,1)S(1)}, u32[]{:S(2)}, u32[]{:S(2)}) collective-permute-start(bf16[128,1792]{1,0:T(8,128)(2,1)S(1)} %fusion.4.refs_5_), channel_id=1, source_target_pairs={{0,64},{1,65},{2,66},{3,67},{4,68},{5,69},{6,70},{7,71},{8,200},{9... | collective-permute-start | bytes 1376264 | tf_op jit(solution)/shard_map/ppermute | solution.py:29
  14.2 13.7 %all-to-all-start = ((bf16[8,24,1024]{2,1,0:T(8,128)(2,1)}), bf16[8,24,1024]{2,1,0:T(8,128)(2,1)S(1)}, u32[]{:S(2)}, u32[]{:S(2)}) async-start(bf16[8,24,1024]{2,1,0:T(8,128)(2,1)} %pad_maximum_fusion.4), calls=%async_computation | async-start | bytes 786432 | tf_op jit(solution)/shard_map/all_to_all | solution.py:219
  18.9 16.9 %copy-start.19 = (f32[2]{0:T(128)S(1)}, f32[2]{0:T(128)}, u32[]{:S(2)}) copy-start(f32[2]{0:T(128)} %param.8) | copy-start | bytes 28
  18.9 9.0 %collective-permute-start.2 = (bf16[128,1792]{1,0:T(8,128)(2,1)S(1)}, bf16[128,1792]{1,0:T(8,128)(2,1)S(1)}, u32[]{:S(2)}, u32[]{:S(2)}) collective-permute-start(bf16[128,1792]{1,0:T(8,128)(2,1)S(1)} %collective-permute-done.1.refs_6_), channel_id=1, source_target_pairs={{0,16},{1,17},{2,18},{3,19},{4,20},{5,21},{6,22},{7,23},{8,56},{9,... | collective-permute-start | bytes 1376264 | tf_op jit(solution)/shard_map/ppermute | solution.py:29
  27.9 7.6 %copy-start.14 = (bf16[128,1792]{1,0:T(8,128)(2,1)}, bf16[128,1792]{1,0:T(8,128)(2,1)S(1)}, u32[]{:S(2)}) copy-start(bf16[128,1792]{1,0:T(8,128)(2,1)S(1)} %collective-permute-done.2.refs_7_) | copy-start | bytes 1376260
  27.9 7.6 %collective-permute-start.5 = (bf16[128,1792]{1,0:T(8,128)(2,1)S(1)}, bf16[128,1792]{1,0:T(8,128)(2,1)S(1)}, u32[]{:S(2)}, u32[]{:S(2)}) collective-permute-start(bf16[128,1792]{1,0:T(8,128)(2,1)S(1)} %collective-permute-done.2.refs_7_), channel_id=1, source_target_pairs={{0,16},{1,17},{2,18},{3,19},{4,20},{5,21},{6,22},{7,23},{8,56},{9,... | collective-permute-start | bytes 1376264 | tf_op jit(solution)/shard_map/ppermute | solution.py:29
  28.4 13.6 %collective-permute-start.3 = (bf16[128,1792]{1,0:T(8,128)(2,1)}, bf16[128,1792]{1,0:T(8,128)(2,1)S(1)}, u32[]{:S(2)}, u32[]{:S(2)}) collective-permute-start(bf16[128,1792]{1,0:T(8,128)(2,1)} %copy-done.13), channel_id=1, source_target_pairs={{0,64},{1,65},{2,66},{3,67},{4,68},{5,69},{6,70},{7,71},{8,200},{9... | collective-permute-start | bytes 1376264 | tf_op jit(solution)/shard_map/ppermute | solution.py:29
  31.1 11.0 %collective-permute-start.4 = (bf16[128,1792]{1,0:T(8,128)(2,1)}, bf16[128,1792]{1,0:T(8,128)(2,1)S(1)}, u32[]{:S(2)}, u32[]{:S(2)}) collective-permute-start(bf16[128,1792]{1,0:T(8,128)(2,1)} %copy-done.13), channel_id=1, source_target_pairs={{0,16},{1,17},{2,18},{3,19},{4,20},{5,21},{6,22},{7,23},{8,56},{9,... | collective-permute-start | bytes 1376264 | tf_op jit(solution)/shard_map/ppermute | solution.py:29
  36.8 16.2 %all-to-all-start.1 = ((bf16[16,24,512]{2,1,0:T(8,128)(2,1)}), bf16[16,24,512]{2,1,0:T(8,128)(2,1)S(1)}, u32[]{:S(2)}, u32[]{:S(2)}) async-start(bf16[16,24,512]{2,1,0:T(8,128)(2,1)} %pad_maximum_fusion.5), calls=%async_computation.1 | async-start | bytes 786432 | tf_op jit(solution)/shard_map/all_to_all | solution.py:236
  42.1 17.6 %copy-start.6 = (bf16[128,1792]{1,0:T(8,128)(2,1)}, bf16[128,1792]{1,0:T(8,128)(2,1)S(1)}, u32[]{:S(2)}) copy-start(bf16[128,1792]{1,0:T(8,128)(2,1)S(1)} %collective-permute-done.3.refs_13_) | copy-start | bytes 1376260
  42.1 17.6 %copy-start.7 = (bf16[128,1792]{1,0:T(8,128)(2,1)}, bf16[128,1792]{1,0:T(8,128)(2,1)S(1)}, u32[]{:S(2)}) copy-start(bf16[128,1792]{1,0:T(8,128)(2,1)S(1)} %collective-permute-done.4.refs_10_) | copy-start | bytes 1376260
  43.2 16.4 %collective-permute-start.6 = (bf16[256,1792]{1,0:T(8,128)(2,1)}, bf16[256,1792]{1,0:T(8,128)(2,1)S(1)}, u32[]{:S(2)}, u32[]{:S(2)}) collective-permute-start(bf16[256,1792]{1,0:T(8,128)(2,1)} %pad_maximum_fusion), channel_id=1, source_target_pairs={{0,16},{1,17},{2,18},{3,19},{4,20},{5,21},{6,22},{7,23},{8,56},{9,... | collective-permute-start | bytes 2752520 | tf_op jit(solution)/shard_map/ppermute | solution.py:29
  45.7 18.4 %collective-permute-start.7 = (bf16[128,1792]{1,0:T(8,128)(2,1)S(1)}, bf16[128,1792]{1,0:T(8,128)(2,1)S(1)}, u32[]{:S(2)}, u32[]{:S(2)}) collective-permute-start(bf16[128,1792]{1,0:T(8,128)(2,1)S(1)} %collective-permute-done.3.refs_13_), channel_id=1, source_target_pairs={{0,64},{1,65},{2,66},{3,67},{4,68},{5,69},{6,70},{7,71},{8,200},{9... | collective-permute-start | bytes 1376264 | tf_op jit(solution)/shard_map/ppermute | solution.py:29
  53.2 14.8 %collective-permute-start.8 = (bf16[272,512]{1,0:T(8,128)(2,1)S(1)}, bf16[272,512]{1,0:T(8,128)(2,1)S(1)}, u32[]{:S(2)}, u32[]{:S(2)}) collective-permute-start(bf16[272,512]{1,0:T(8,128)(2,1)S(1)} %get-tuple-element.47), channel_id=1, source_target_pairs={{0,4},{1,5},{2,6},{3,7},{4,0},{5,1},{6,2},{7,3},{8,12},{9,13},{10,... | collective-permute-start | bytes 835592 | tf_op jit(solution)/shard_map/ppermute | solution.py:29
  59.6 4.6 %copy-start = (bf16[256,1792]{1,0:T(8,128)(2,1)}, bf16[256,1792]{1,0:T(8,128)(2,1)S(1)}, u32[]{:S(2)}) copy-start(bf16[256,1792]{1,0:T(8,128)(2,1)S(1)} %collective-permute-done.6.refs_11_.refs_14_) | copy-start | bytes 2752516
  59.7 12.6 %copy-start.16 = (bf16[128,1792]{1,0:T(8,128)(2,1)S(1)}, bf16[128,1792]{1,0:T(8,128)(2,1)}, u32[]{:S(2)}) copy-start(bf16[128,1792]{1,0:T(8,128)(2,1)} %copy-done.15) | copy-start | bytes 1376260
  64.1 9.1 %copy-start.8 = (bf16[128,1792]{1,0:T(8,128)(2,1)}, bf16[128,1792]{1,0:T(8,128)(2,1)S(1)}, u32[]{:S(2)}) copy-start(bf16[128,1792]{1,0:T(8,128)(2,1)S(1)} %collective-permute-done.7.refs_17_) | copy-start | bytes 1376260
  68.1 35.1 %copy-start.4 = (bf16[2,272,512]{2,1,0:T(8,128)(2,1)}, bf16[2,272,512]{2,1,0:T(8,128)(2,1)S(1)}, u32[]{:S(2)}) copy-start(bf16[2,272,512]{2,1,0:T(8,128)(2,1)S(1)} %pad_maximum_fusion.3.refs_1_) | copy-start | bytes 1671172
  68.1 13.1 %collective-permute-start.10 = (bf16[256,1792]{1,0:T(8,128)(2,1)S(1)}, bf16[256,1792]{1,0:T(8,128)(2,1)S(1)}, u32[]{:S(2)}, u32[]{:S(2)}) collective-permute-start(bf16[256,1792]{1,0:T(8,128)(2,1)S(1)} %pad_maximum_fusion.1), channel_id=1, source_target_pairs={{0,16},{1,17},{2,18},{3,19},{4,20},{5,21},{6,22},{7,23},{8,56},{9,... | collective-permute-start | bytes 2752520 | tf_op jit(solution)/shard_map/ppermute | solution.py:29
  70.8 15.9 %collective-permute-start.12 = (bf16[2,272,512]{2,1,0:T(8,128)(2,1)S(1)}, bf16[2,272,512]{2,1,0:T(8,128)(2,1)S(1)}, u32[]{:S(2)}, u32[]{:S(2)}) collective-permute-start(bf16[2,272,512]{2,1,0:T(8,128)(2,1)S(1)} %pad_maximum_fusion.3.refs_1_), channel_id=1, source_target_pairs={{0,3},{1,0},{2,1},{3,2},{4,7},{5,4},{6,5},{7,6},{8,11},{9,8},{10,9... | collective-permute-start | bytes 1671176 | tf_op jit(solution)/shard_map/ppermute | solution.py:29
  71.2 15.4 %collective-permute-start.11 = (bf16[2,272,512]{2,1,0:T(8,128)(2,1)S(1)}, bf16[2,272,512]{2,1,0:T(8,128)(2,1)S(1)}, u32[]{:S(2)}, u32[]{:S(2)}) collective-permute-start(bf16[2,272,512]{2,1,0:T(8,128)(2,1)S(1)} %pad_maximum_fusion.3.refs_1_), channel_id=1, source_target_pairs={{0,1},{1,2},{2,3},{3,0},{4,5},{5,6},{6,7},{7,4},{8,9},{9,10},{10,1... | collective-permute-start | bytes 1671176 | tf_op jit(solution)/shard_map/ppermute | solution.py:29
  72.3 14.4 %collective-permute-start.9 = (bf16[128,1792]{1,0:T(8,128)(2,1)S(1)}, bf16[128,1792]{1,0:T(8,128)(2,1)S(1)}, u32[]{:S(2)}, u32[]{:S(2)}) collective-permute-start(bf16[128,1792]{1,0:T(8,128)(2,1)S(1)} %copy-done.16), channel_id=1, source_target_pairs={{0,192},{1,193},{2,194},{3,195},{4,196},{5,197},{6,198},{7,199},{8... | collective-permute-start | bytes 1376264 | tf_op jit(solution)/shard_map/ppermute | solution.py:29
  81.2 21.9 %copy-start.2 = (bf16[256,1792]{1,0:T(8,128)(2,1)}, bf16[256,1792]{1,0:T(8,128)(2,1)S(1)}, u32[]{:S(2)}) copy-start(bf16[256,1792]{1,0:T(8,128)(2,1)S(1)} %collective-permute-done.10.refs_15_.refs_18_) | copy-start | bytes 2752516
  86.7 15.2 %copy-start.17 = (bf16[128,1792]{1,0:T(8,128)(2,1)}, bf16[128,1792]{1,0:T(8,128)(2,1)S(1)}, u32[]{:S(2)}) copy-start(bf16[128,1792]{1,0:T(8,128)(2,1)S(1)} %collective-permute-done.9.refs_20_) | copy-start | bytes 1376260
  86.7 16.5 %collective-permute-start.14 = (bf16[256,1792]{1,0:T(8,128)(2,1)}, bf16[256,1792]{1,0:T(8,128)(2,1)S(1)}, u32[]{:S(2)}, u32[]{:S(2)}) collective-permute-start(bf16[256,1792]{1,0:T(8,128)(2,1)} %pad_maximum_fusion.2), channel_id=1, source_target_pairs={{0,16},{1,17},{2,18},{3,19},{4,20},{5,21},{6,22},{7,23},{8,56},{9,... | collective-permute-start | bytes 2752520 | tf_op jit(solution)/shard_map/ppermute | solution.py:29
  87.6 14.3 %collective-permute-start.15 = (bf16[128,1792]{1,0:T(8,128)(2,1)S(1)}, bf16[128,1792]{1,0:T(8,128)(2,1)S(1)}, u32[]{:S(2)}, u32[]{:S(2)}) collective-permute-start(bf16[128,1792]{1,0:T(8,128)(2,1)S(1)} %collective-permute-done.9.refs_20_), channel_id=1, source_target_pairs={{0,192},{1,193},{2,194},{3,195},{4,196},{5,197},{6,198},{7,199},{8... | collective-permute-start | bytes 1376264 | tf_op jit(solution)/shard_map/ppermute | solution.py:29
  88.3 14.9 %collective-permute-start.13 = (bf16[2,272,512]{2,1,0:T(8,128)(2,1)S(1)}, bf16[2,272,512]{2,1,0:T(8,128)(2,1)}, u32[]{:S(2)}, u32[]{:S(2)}) collective-permute-start(bf16[2,272,512]{2,1,0:T(8,128)(2,1)S(1)} %pad_maximum_fusion.3.refs_1_), channel_id=1, source_target_pairs={{0,2},{1,3},{2,0},{3,1},{4,6},{5,7},{6,4},{7,5},{8,10},{9,11},{10,... | collective-permute-start | bytes 1671176 | tf_op jit(solution)/shard_map/ppermute | solution.py:29
  103.2 16.0 %copy-start.9 = (bf16[256,1792]{1,0:T(8,128)(2,1)S(1)}, bf16[256,1792]{1,0:T(8,128)(2,1)}, u32[]{:S(2)}) copy-start(bf16[256,1792]{1,0:T(8,128)(2,1)} %param.9) | copy-start | bytes 2752516
  113.7 5.5 %collective-permute-start.16 = (f32[256,1792]{1,0:T(8,128)}, f32[256,1792]{1,0:T(8,128)S(1)}, u32[]{:S(2)}, u32[]{:S(2)}) collective-permute-start(f32[256,1792]{1,0:T(8,128)} %get-tuple-element.41), channel_id=1, source_target_pairs={{0,8},{1,9},{2,10},{3,11},{4,12},{5,13},{6,14},{7,15},{8,0},{9,1},... | collective-permute-start | bytes 5505032 | tf_op jit(solution)/shard_map/ppermute | solution.py:29
  (7 other events, 10.1 us)
